TPU v7x, 512 devices: a whole 4x8x8 slice. The times are simulated.
512 devices in a mesh: ctx: 64 (over z, y), head: 8 (over x, core).
Axes of the slice: x: 4, y: 8, z: 8, core: 2. Of those that a mesh axis runs over, the one named last changes fastest.
Arguments:
- queries: bfloat16 [32768, 4096], P(('ctx', 'head')), may hold values from -0.625 to 0.625
- keys: bfloat16 [32768, 4096], P(('ctx', 'head')), may hold values from -0.625 to 0.625
- values: bfloat16 [32768, 4096], P(('ctx', 'head')), may hold values from -0.625 to 0.625
- out_grad: bfloat16 [32768, 4096], P(('ctx', 'head')), may hold values from -0.625 to 0.625
- doc_ids: int32 [32768], replicated, may hold values from 0 to 7, as said below
Outputs:
- attended: bfloat16 [32768, 4096], P('ctx', 'head')
- grad_queries: bfloat16 [32768, 4096], P('ctx', 'head')
- grad_keys: bfloat16 [32768, 4096], P('ctx', 'head')
- grad_values: bfloat16 [32768, 4096], P('ctx', 'head')
Inputs may be any that keep to these rules, and one draw needn't show every extreme that they name: `doc_ids`: document ids start at 0, never fall along the window and rise by one at each document start; all 8 documents occur, each holds 1 to 16384 tokens, one exactly 16384.
All inputs are finite; a program needn't handle non-finite values.
Results may differ from a plain program's by a relative error of at most 0.015.
Values may be sent and summed in bfloat16 or wider, within the bound.
A program may use at most 128 MiB of HBM per device.

v0:
```python
import jax
import jax.numpy as jnp
from jax import lax
from jax.sharding import PartitionSpec as P

DH = 128


def prefix_2(value, axis, join, neutral, backward):
    count, mine = (lax.axis_size(axis), lax.axis_index(axis))
    pieces = jax.tree.map(lambda part: lax.all_gather(part, axis), value)
    if backward:
        pieces = jax.tree.map(lambda part: part[::-1], pieces)
        mine = count - 1 - mine
    running = jax.tree.map(
        lambda part, zero: jnp.full_like(part, 0) + jnp.asarray(zero, part.dtype), value, neutral
    )

    def turn(position, running):
        longer = join(running, jax.tree.map(lambda part: part[position], pieces))
        return jax.tree.map(lambda new, old: jnp.where(position < mine, new, old), longer, running)

    return lax.fori_loop(0, count - 1, turn, running)


def combine_state(earlier, later):
    return (later[0] + later[1] * earlier[0], earlier[1] * later[1])


def head_major(array, tok_rows, head_count):
    return jnp.transpose(array.reshape(tok_rows, head_count, DH), (1, 0, 2))


def token_major(array, tok_rows, head_count):
    return jnp.transpose(array, (1, 0, 2)).reshape(tok_rows, head_count * DH)


def shards(queries, keys, values, out_grad, doc_ids):
    queries, keys, values, out_grad = (
        lax.all_to_all(queries, "head", split_axis=1, concat_axis=0, tiled=True),
        lax.all_to_all(keys, "head", split_axis=1, concat_axis=0, tiled=True),
        lax.all_to_all(values, "head", split_axis=1, concat_axis=0, tiled=True),
        lax.all_to_all(out_grad, "head", split_axis=1, concat_axis=0, tiled=True),
    )
    tok_rows = queries.shape[0]
    head_count = queries.shape[1] // DH
    query_heads = head_major(queries, tok_rows, head_count)
    key_heads = head_major(keys, tok_rows, head_count)
    value_heads = head_major(values, tok_rows, head_count)
    grad_heads = head_major(out_grad, tok_rows, head_count)
    window = doc_ids.shape[0]
    offset = lax.axis_index("ctx") * tok_rows
    local_docs = lax.dynamic_slice_in_dim(doc_ids, offset, tok_rows)
    prior_doc = lax.dynamic_slice_in_dim(doc_ids, jnp.maximum(offset - 1, 0), 1)[0]
    next_doc = lax.dynamic_slice_in_dim(doc_ids, jnp.minimum(offset + tok_rows, window - 1), 1)[0]
    prior_doc = jnp.where(offset == 0, jnp.int32(-1), prior_doc)
    next_doc = jnp.where(offset + tok_rows >= window, jnp.int32(-1), next_doc)
    positions = jnp.arange(tok_rows)
    allowed = (positions[:, None] >= positions[None, :]) & (
        local_docs[:, None] == local_docs[None, :]
    )
    scores = jnp.einsum("htd,hsd->hts", query_heads, key_heads, preferred_element_type=jnp.float32)
    scores = jnp.where(allowed[None], scores, 0.0).astype(jnp.bfloat16)
    dscores = jnp.einsum(
        "htd,hsd->hts", grad_heads, value_heads, preferred_element_type=jnp.float32
    )
    dscores = jnp.where(allowed[None], dscores, 0.0).astype(jnp.bfloat16)
    last_doc = local_docs[-1]
    first_doc = local_docs[0]
    tail_mask = (local_docs == last_doc).astype(jnp.bfloat16)[None, :, None]
    lead_mask = (local_docs == first_doc).astype(jnp.bfloat16)[None, :, None]
    state_local = jnp.einsum(
        "hti,htj->hij", key_heads * tail_mask, value_heads, preferred_element_type=jnp.float32
    )
    keep_fwd = (last_doc == prior_doc).astype(jnp.float32)
    keep_bwd = (first_doc == next_doc).astype(jnp.float32)
    empty_state = jnp.zeros((head_count, DH, DH), jnp.float32)
    unity = jnp.ones((), jnp.float32)
    prefix, spent = prefix_2(
        (state_local, keep_fwd), "ctx", combine_state, (empty_state, unity), False
    )
    grad_local = jnp.einsum(
        "hti,htj->hij", query_heads * lead_mask, grad_heads, preferred_element_type=jnp.float32
    )
    suffix, unused = prefix_2(
        (grad_local, keep_bwd), "ctx", combine_state, (empty_state, unity), True
    )
    held = prefix.astype(jnp.bfloat16)
    gheld = suffix.astype(jnp.bfloat16)
    match = (local_docs == prior_doc).astype(jnp.float32)[None, :, None]
    back = (local_docs == next_doc).astype(jnp.float32)[None, :, None]
    attended = jnp.einsum("hts,hsd->htd", scores, value_heads, preferred_element_type=jnp.float32)
    attended = attended + match * jnp.einsum(
        "hti,hij->htj", query_heads, held, preferred_element_type=jnp.float32
    )
    grad_query = jnp.einsum("hts,hsd->htd", dscores, key_heads, preferred_element_type=jnp.float32)
    grad_query = grad_query + match * jnp.einsum(
        "htj,hij->hti", grad_heads, held, preferred_element_type=jnp.float32
    )
    grad_key = jnp.einsum("hts,htd->hsd", dscores, query_heads, preferred_element_type=jnp.float32)
    grad_key = grad_key + back * jnp.einsum(
        "hsj,hij->hsi", value_heads, gheld, preferred_element_type=jnp.float32
    )
    grad_value = jnp.einsum("hts,htj->hsj", scores, grad_heads, preferred_element_type=jnp.float32)
    grad_value = grad_value + back * jnp.einsum(
        "hsi,hij->hsj", key_heads, gheld, preferred_element_type=jnp.float32
    )
    return (
        token_major(attended.astype(jnp.bfloat16), tok_rows, head_count),
        token_major(grad_query.astype(jnp.bfloat16), tok_rows, head_count),
        token_major(grad_key.astype(jnp.bfloat16), tok_rows, head_count),
        token_major(grad_value.astype(jnp.bfloat16), tok_rows, head_count),
    )


def solution(mesh):
    placed = (
        P(("ctx", "head"), None),
        P(("ctx", "head"), None),
        P(("ctx", "head"), None),
        P(("ctx", "head"), None),
        P(),
    )
    return jax.shard_map(
        shards,
        mesh=mesh,
        in_specs=placed,
        out_specs=(P("ctx", "head"), P("ctx", "head"), P("ctx", "head"), P("ctx", "head")),
        check_vma=False,
    )
```

profile of v0, /device:TPU:2, one launch (start us, length us, event | category | flops | bytes accessed | tf_op | source)
XLA Modules:
  0.0 561.9 jit_solution(16993205234866495056)
XLA Ops:
  7.2 1.9 copy.149
  9.1 9.3 %all-to-all-start = ((bf16[64,8,512]{2,0,1:T(8,128)(2,1)}), bf16[64,8,512]{2,0,1:T(8,128)(2,1)S(1)}, u32[]{:S(2)}, u32[]{:S(2)}) async-start(bf16[64,8,512]{2,0,1:T(8,128)(2,1)} %bitcast.126), calls=%async_computation | async-start | bytes 1048576 | tf_op jit(solution)/shard_map/all_to_all | solution.py:40
  19.3 8.1 %all-to-all-done = bf16[64,8,512]{2,0,1:T(8,128)(2,1)S(1)} async-done(((bf16[64,8,512]{2,0,1:T(8,128)(2,1)}), bf16[64,8,512]{2,0,1:T(8,128)(2,1)S(1)}, u32[]{:S(2)}, u32[]{:S(2)}) %all-to-all-start) | async-done | bytes 524320 | tf_op jit(solution)/shard_map/all_to_all | solution.py:40
  27.3 4.9 all-to-all-start.3
  37.7 3.4 all-to-all-done.3
  43.3 4.9 all-to-all-start.2
  49.0 8.1 %all-to-all-done.2 = bf16[64,8,512]{2,0,1:T(8,128)(2,1)S(1)} async-done(((bf16[64,8,512]{2,0,1:T(8,128)(2,1)}), bf16[64,8,512]{2,0,1:T(8,128)(2,1)S(1)}, u32[]{:S(2)}, u32[]{:S(2)}) %all-to-all-start.2) | async-done | bytes 524320 | tf_op jit(solution)/shard_map/all_to_all | solution.py:42
  57.1 4.9 all-to-all-start.1
  62.4 8.5 %all-to-all-done.1 = bf16[64,8,512]{2,0,1:T(8,128)(2,1)S(1)} async-done(((bf16[64,8,512]{2,0,1:T(8,128)(2,1)}), bf16[64,8,512]{2,0,1:T(8,128)(2,1)S(1)}, u32[]{:S(2)}, u32[]{:S(2)}) %all-to-all-start.1) | async-done | bytes 524320 | tf_op jit(solution)/shard_map/all_to_all | solution.py:41
  76.2 147.3 %all-reduce.2 = (f32[64]{0:T(128)S(1)}, f32[64]{0:T(128)S(1)}) all-reduce(f32[64]{0:T(128)S(1)} %dynamic-update-slice, f32[64]{0:T(128)S(1)} %dynamic-update-slice.1), channel_id=1, replica_groups=mesh['ctx'=64,'head'=8] {'ctx'}, use_global_device_ids=true, to_apply=%add | all-reduce | flops 128 | bytes 1024
  226.9 1.8 convolution_bitcast_fusion.2
  232.0 11.8 %rev.6 = f32[64,4,128,128]{3,2,1,0:T(8,128)} reverse(f32[64,4,128,128]{3,2,1,0:T(8,128)} %bitcast.135), dimensions={0} | reverse | bytes 33554432 | tf_op jit(solution)/shard_map/rev | solution.py:13
  243.8 150.9 %while.29 = (s32[]{:T(128)}, f32[4,128,128]{2,1,0:T(8,128)S(1)}, s32[]{:T(128)}, f32[64,4,128,128]{3,2,1,0:T(8,128)}, f32[64]{0:T(128)S(1)}, /*index=5*/s32[]{:T(128)}, s32[]{:T(128)}) while((s32[]{:T(128)}, f32[4,128,128]{2,1,0:T(8,128)S(1)}, s32[]{:T(128)}, f32[64,4,128,128]{3,2,1,0:T(8,128)}, f32[64]{0:T(128)S(1)}, ...), condition=%wide.region_3.4_spmd.clone, body=%wide.region_2.3_spmd.clone.sunk | while | flops 262148 | bytes 786549 | solution.py:23
  244.3 1.8 fusion.58
  246.7 1.8 fusion.58
  249.1 1.8 fusion.58
  251.5 1.8 fusion.58
  253.9 1.8 fusion.58
  256.3 1.8 fusion.58
  258.7 1.8 fusion.58
  261.1 1.8 fusion.58
  263.5 1.8 fusion.58
  265.9 1.8 fusion.58
  268.3 1.8 fusion.58
  270.7 1.8 fusion.58
  273.1 1.8 fusion.58
  275.5 1.8 fusion.58
  277.9 1.8 fusion.58
  280.3 1.8 fusion.58
  282.7 1.8 fusion.58
  285.1 1.8 fusion.58
  287.5 1.8 fusion.58
  289.9 1.8 fusion.58
  292.3 1.8 fusion.58
  294.7 1.8 fusion.58
  297.1 1.8 fusion.58
  299.5 1.8 fusion.58
  301.9 1.8 fusion.58
  304.3 1.8 fusion.58
  306.7 1.8 fusion.58
  309.1 1.8 fusion.58
  311.5 1.8 fusion.58
  313.9 1.8 fusion.58
  316.3 1.8 fusion.58
  318.7 1.8 fusion.58
  321.1 1.8 fusion.58
  323.5 1.8 fusion.58
  325.9 1.8 fusion.58
  328.3 1.8 fusion.58
  330.7 1.8 fusion.58
  333.1 1.8 fusion.58
  335.5 1.8 fusion.58
  337.8 1.8 fusion.58
  340.2 1.8 fusion.58
  342.6 1.8 fusion.58
  345.0 1.8 fusion.58
  347.4 1.8 fusion.58
  349.8 1.8 fusion.58
  352.2 1.8 fusion.58
  354.6 1.8 fusion.58
  357.0 1.8 fusion.58
  359.4 1.8 fusion.58
  399.8 150.7 %while.28 = (s32[]{:T(128)}, f32[4,128,128]{2,1,0:T(8,128)S(1)}, s32[]{:T(128)}, f32[64,4,128,128]{3,2,1,0:T(8,128)}, f32[64]{0:T(128)S(1)}, /*index=5*/s32[]{:T(128)}, s32[]{:T(128)}) while((s32[]{:T(128)}, f32[4,128,128]{2,1,0:T(8,128)S(1)}, s32[]{:T(128)}, f32[64,4,128,128]{3,2,1,0:T(8,128)}, f32[64]{0:T(128)S(1)}, ...), condition=%wide.region_1.2_spmd.clone, body=%wide.region_0.1_spmd.clone.sunk | while | flops 262148 | bytes 786549 | solution.py:23
  551.6 2.0 copy.65
  (254 shorter events, 238.4 us)
Async XLA Ops:
  7.2 11.3 %copy-start.2 = (bf16[64,4096]{1,0:T(8,128)(2,1)S(1)}, bf16[64,4096]{1,0:T(8,128)(2,1)}, u32[]{:S(2)}) copy-start(bf16[64,4096]{1,0:T(8,128)(2,1)} %param.12) | copy-start | bytes 1572868
  9.1 18.2 %all-to-all-start = ((bf16[64,8,512]{2,0,1:T(8,128)(2,1)}), bf16[64,8,512]{2,0,1:T(8,128)(2,1)S(1)}, u32[]{:S(2)}, u32[]{:S(2)}) async-start(bf16[64,8,512]{2,0,1:T(8,128)(2,1)} %bitcast.126), calls=%async_computation | async-start | bytes 1048576 | tf_op jit(solution)/shard_map/all_to_all | solution.py:40
  27.3 13.8 %all-to-all-start.3 = ((bf16[64,8,512]{2,0,1:T(8,128)(2,1)}), bf16[64,8,512]{2,0,1:T(8,128)(2,1)S(1)}, u32[]{:S(2)}, u32[]{:S(2)}) async-start(bf16[64,8,512]{2,0,1:T(8,128)(2,1)} %bitcast.123), calls=%async_computation.3 | async-start | bytes 1048576 | tf_op jit(solution)/shard_map/all_to_all | solution.py:43
  32.2 10.2 %copy-start.3 = (bf16[64,4096]{1,0:T(8,128)(2,1)S(1)}, bf16[64,4096]{1,0:T(8,128)(2,1)}, u32[]{:S(2)}) copy-start(bf16[64,4096]{1,0:T(8,128)(2,1)} %param.11) | copy-start | bytes 1572868
  32.2 199.8 %all-gather.7.cloned.1.call-start = ((), (), s32[]{:S(2)}) async-start(), calls=%async_computation.5 | async-start | bytes 17039360 | tf_op jit(solution)/shard_map/all_gather | solution.py:11
  41.2 6.9 %copy-start.4 = (bf16[64,4096]{1,0:T(8,128)(2,1)S(1)}, bf16[64,4096]{1,0:T(8,128)(2,1)}, u32[]{:S(2)}) copy-start(bf16[64,4096]{1,0:T(8,128)(2,1)} %param.10) | copy-start | bytes 1572868
  43.3 13.8 %all-to-all-start.2 = ((bf16[64,8,512]{2,0,1:T(8,128)(2,1)}), bf16[64,8,512]{2,0,1:T(8,128)(2,1)S(1)}, u32[]{:S(2)}, u32[]{:S(2)}) async-start(bf16[64,8,512]{2,0,1:T(8,128)(2,1)} %bitcast.124), calls=%async_computation.2 | async-start | bytes 1048576 | tf_op jit(solution)/shard_map/all_to_all | solution.py:42
  57.1 13.8 %all-to-all-start.1 = ((bf16[64,8,512]{2,0,1:T(8,128)(2,1)}), bf16[64,8,512]{2,0,1:T(8,128)(2,1)S(1)}, u32[]{:S(2)}, u32[]{:S(2)}) async-start(bf16[64,8,512]{2,0,1:T(8,128)(2,1)} %bitcast.125), calls=%async_computation.1 | async-start | bytes 1048576 | tf_op jit(solution)/shard_map/all_to_all | solution.py:41
  61.9 337.9 %all-gather.5.cloned.1.call-start = ((), (), s32[]{:S(2)}) async-start(), calls=%async_computation.4 | async-start | bytes 17039360 | tf_op jit(solution)/shard_map/all_gather | solution.py:11
  398.8 151.8 %copy-start.1 = (f32[512,4,128]{0,2,1:T(8,128)S(1)}, f32[512,4,128]{0,2,1:T(8,128)}, u32[]{:S(2)}) copy-start(f32[512,4,128]{0,2,1:T(8,128)} %convolution_bitcast_fusion.2) | copy-start | bytes 3145732
  550.5 3.2 copy-start
Sparse Core Ops, SparseCore 0:
  42.6 140.9 all-gather.6
  187.2 138.0 all-gather.4
where the time goes:
time: 568 us; the launch traced here: 562 us
  other arithmetic  228 us (40%)
  blocking collectives  147 us (26%)
  local copies, waits for them, and re-layouts  101 us (18%)
  waiting for transfers between devices  28.1 us (5%)
  starting transfers between devices  23.9 us (4%)
  between operations  16.8 us (3%)
  matrix products  15 us (3%)
    select_n x126, other arithmetic, turn(): jnp.where(position < mine, new, old)  226 us
    unnamed x1, blocking collectives  147 us
    dynamic_slice x126, local copies, waits for them, and re-layouts, turn(): longer = join(running, jax.tree.map(lambda part: part[position], pieces))  73.9 us
    rev x2, local copies, waits for them, and re-layouts, prefix_2(): pieces = jax.tree.map(lambda part: part[::-1], pieces)  11.9 us
  transfers between devices with their start and end apart: 6, of which 4 were waited for; matrix products, arithmetic and copies ran while one was open for 33% of the time, Pallas kernels for 0%

commit v1 on v0

v1 whole, which is shorter than its diff:
```python
import functools

import jax
import jax.numpy as jnp
from jax import lax
from jax.experimental import pallas as pl
from jax.experimental.pallas import tpu as pltpu
from jax.sharding import PartitionSpec as P

DH = 128
ROW = 8
MESH = pl.DeviceIdType.MESH
F32, BF16 = jnp.float32, jnp.bfloat16
K, V, Q, G = range(4)


def nt(a, b):
    return lax.dot_general(a, b, (((1,), (1,)), ((), ())), preferred_element_type=F32)


def nn(a, b):
    return lax.dot_general(a, b, (((1,), (0,)), ((), ())), preferred_element_type=F32)


def tn(a, b):
    return lax.dot_general(a, b, (((0,), (0,)), ((), ())), preferred_element_type=F32)


def one_if(flag):
    return jnp.where(flag, F32(1.0), F32(0.0))


def kernel(
    nx, ny, nz, heads, tok,
    q_ref, k_ref, v_ref, g_ref, docs_ref,
    att_ref, gq_ref, gk_ref, gv_ref,
    buf, acc, allow, allow_t, cols, docs_v, docs_s,
    st, y_in, z_out, z_in, p_out, held,
    docs_sem, own_sem, a_send, a_recv, y_send, y_recv, z_send, z_recv, p_send, p_recv,
):
    ctx = lax.axis_index("ctx")
    me_x = lax.axis_index("head")
    me_z, me_y = ctx // ny, ctx % ny
    part = tok // nx
    rows = DH // ny
    per = tok // 128
    blocks = ny * nz

    def x_peer(step):
        return lax.rem(me_x + step, nx)

    def y_peer(step):
        return lax.rem(me_y + step, ny)

    def z_peer(step):
        return lax.rem(me_z + step, nz)

    docs_copies = [
        pltpu.make_async_copy(docs_ref, docs_s, docs_sem.at[0]),
        pltpu.make_async_copy(docs_ref, docs_v, docs_sem.at[1]),
    ]
    for copy in docs_copies:
        copy.start()

    barrier = pltpu.get_barrier_semaphore()
    for step in range(1, nx):
        pl.semaphore_signal(barrier, inc=1, device_id={"head": x_peer(step)}, device_id_type=MESH)
    for step in range(1, ny):
        pl.semaphore_signal(barrier, inc=1, device_id={"ctx": me_z * ny + y_peer(step)}, device_id_type=MESH)
    for step in range(1, nz):
        pl.semaphore_signal(barrier, inc=1, device_id={"ctx": z_peer(step) * ny + me_y}, device_id_type=MESH)
    pl.semaphore_wait(barrier, nx + ny + nz - 3)

    sources = (k_ref, v_ref, q_ref, g_ref)
    mine = pl.ds(pl.multiple_of(me_x * part, part), part)

    def columns(owner, h):
        return pl.ds(pl.multiple_of((owner * heads + h) * DH, DH), DH)

    def send_tokens(h, carry):
        for a in range(4):
            pltpu.make_async_copy(
                sources[a].at[:, columns(me_x, h)], buf.at[a, h, mine, :], own_sem.at[a, h]
            ).start()
            for step in range(1, nx):
                peer = x_peer(step)
                pltpu.make_async_remote_copy(
                    src_ref=sources[a].at[:, columns(peer, h)],
                    dst_ref=buf.at[a, h, mine, :],
                    send_sem=a_send.at[a, h],
                    recv_sem=a_recv.at[a, h],
                    device_id={"head": peer},
                    device_id_type=MESH,
                ).start()
        return carry

    lax.fori_loop(0, heads, send_tokens, 0)

    def wait_bytes(ref, sem):
        pltpu.make_async_copy(ref, ref, sem).wait()

    for copy in docs_copies:
        copy.wait()

    def last(block):
        return docs_s[block * per + per - 1, 127]

    def first(block):
        return docs_s[block * per, 0]

    prior_doc = jnp.where(ctx == 0, -1, last(jnp.maximum(ctx - 1, 0)))
    next_doc = jnp.where(ctx == blocks - 1, -1, first(jnp.minimum(ctx + 1, blocks - 1)))
    last_doc, first_doc = last(ctx), first(ctx)

    local = docs_v[pl.ds(pl.multiple_of(ctx * per, per), per), :]
    row_of = [jnp.broadcast_to(local[i : i + 1, :], (128, 128)) for i in range(per)]
    col_of = [r.T for r in row_of]
    t_pos = lax.broadcasted_iota(jnp.int32, (128, 128), 0)
    s_pos = lax.broadcasted_iota(jnp.int32, (128, 128), 1)
    for i in range(per):
        at = slice(i * 128, (i + 1) * 128)
        for n, doc in enumerate((last_doc, first_doc, prior_doc, next_doc)):
            cols[n, at, :] = one_if(col_of[i] == doc).astype(BF16)
        for j in range(per):
            to = slice(j * 128, (j + 1) * 128)
            same = col_of[i] == row_of[j]
            allow[at, to] = one_if(same & (t_pos + i * 128 >= s_pos + j * 128)).astype(BF16)
            allow_t[at, to] = one_if(same & (t_pos + i * 128 <= s_pos + j * 128)).astype(BF16)

    tile = min(256, tok)

    def intra(h, left, right, by_row, by_col):
        for i in range(tok // tile):
            at, upto = slice(i * tile, (i + 1) * tile), slice(0, (i + 1) * tile)
            s = nt(buf[left, h, at, :], buf[right, h, upto, :]).astype(BF16) * allow[at, upto]
            acc[by_row[0], h, at, :] = nn(s, buf[by_row[1], h, upto, :])
            onward = slice(i * tile, tok)
            s = nt(buf[right, h, at, :], buf[left, h, onward, :]).astype(BF16) * allow_t[at, onward]
            acc[by_col[0], h, at, :] = nn(s, buf[by_col[1], h, onward, :])

    def stage_states(h):
        for a in (K, V):
            wait_bytes(buf.at[a, h, pl.ds(0, part), :], own_sem.at[a, h])
            wait_bytes(buf.at[a, h, pl.ds(0, tok - part), :], a_recv.at[a, h])
        st[h, 0] = tn(buf[K, h] * cols[0], buf[V, h]).astype(BF16)
        for a in (Q, G):
            wait_bytes(buf.at[a, h, pl.ds(0, part), :], own_sem.at[a, h])
            wait_bytes(buf.at[a, h, pl.ds(0, tok - part), :], a_recv.at[a, h])
        st[h, 1] = tn(buf[Q, h] * cols[1], buf[G, h]).astype(BF16)
        for step in range(1, ny):
            peer = y_peer(step)
            pltpu.make_async_remote_copy(
                src_ref=st.at[h, :, pl.ds(pl.multiple_of(peer * rows, rows), rows), :],
                dst_ref=y_in.at[h, me_y],
                send_sem=y_send.at[h],
                recv_sem=y_recv.at[h],
                device_id={"ctx": me_z * ny + peer},
                device_id_type=MESH,
            ).start()
        y_in[h, me_y] = st[h, :, pl.ds(pl.multiple_of(me_y * rows, rows), rows), :]

    def stage_totals(h):
        wait_bytes(y_in.at[h, pl.ds(0, ny - 1)], y_recv.at[h])
        base = me_z * ny
        total = y_in[h, 0, 0].astype(F32)
        for y in range(1, ny):
            keep = one_if(last(base + y) == last(base + y - 1))
            total = y_in[h, y, 0].astype(F32) + keep * total
        z_out[h, 0] = total.astype(BF16)
        total = y_in[h, ny - 1, 1].astype(F32)
        for y in reversed(range(ny - 1)):
            keep = one_if(first(base + y) == first(base + y + 1))
            total = y_in[h, y, 1].astype(F32) + keep * total
        z_out[h, 1] = total.astype(BF16)
        for step in range(1, nz):
            pltpu.make_async_remote_copy(
                src_ref=z_out.at[h, (me_z + step) // nz],
                dst_ref=z_in.at[h, me_z],
                send_sem=z_send.at[h],
                recv_sem=z_recv.at[h],
                device_id={"ctx": z_peer(step) * ny + me_y},
                device_id_type=MESH,
            ).start()
        z_in[h, me_z] = jnp.zeros((rows, DH), BF16)

    def stage_prefix(h):
        wait_bytes(z_in.at[h, pl.ds(0, nz - 1)], z_recv.at[h])
        base = me_z * ny
        before = last(jnp.maximum(base - 1, 0))
        after = first(jnp.minimum(base + ny, blocks - 1))
        state = jnp.zeros((rows, DH), F32)
        gstate = jnp.zeros((rows, DH), F32)
        for z in range(nz):
            term = z_in[h, z].astype(F32)
            state = state + one_if((z < me_z) & (last(z * ny + ny - 1) == before)) * term
            gstate = gstate + one_if((z > me_z) & (first(z * ny) == after)) * term
        for y in range(ny):
            p_out[h, y, 0] = state.astype(BF16)
            if y < ny - 1:
                keep = one_if(last(base + y) == last(jnp.maximum(base + y - 1, 0)))
                state = y_in[h, y, 0].astype(F32) + keep * state
        for y in reversed(range(ny)):
            p_out[h, y, 1] = gstate.astype(BF16)
            if y > 0:
                keep = one_if(first(base + y) == first(jnp.minimum(base + y + 1, blocks - 1)))
                gstate = y_in[h, y, 1].astype(F32) + keep * gstate
        here = pl.ds(pl.multiple_of(me_y * rows, rows), rows)
        for step in range(1, ny):
            peer = y_peer(step)
            pltpu.make_async_remote_copy(
                src_ref=p_out.at[h, peer],
                dst_ref=held.at[h, :, here, :],
                send_sem=p_send.at[h],
                recv_sem=p_recv.at[h],
                device_id={"ctx": me_z * ny + peer},
                device_id_type=MESH,
            ).start()
        held[h, :, here, :] = p_out[h, me_y]

    def stage_finish(h):
        wait_bytes(y_in.at[h, pl.ds(0, ny - 1)], p_recv.at[h])
        to = pl.ds(pl.multiple_of(h * DH, DH), DH)
        state, gstate = held[h, 0], held[h, 1]
        att_ref[:, to] = (acc[0, h] + nn(buf[Q, h] * cols[2], state)).astype(BF16)
        gq_ref[:, to] = (acc[1, h] + nt(buf[G, h] * cols[2], state)).astype(BF16)
        gk_ref[:, to] = (acc[2, h] + nt(buf[V, h] * cols[3], gstate)).astype(BF16)
        gv_ref[:, to] = (acc[3, h] + nn(buf[K, h] * cols[3], gstate)).astype(BF16)

    def turn(h, carry):
        pl.when(h < heads)(lambda: stage_states(h))
        pl.when(h > 0)(lambda: stage_prefix(h - 1))

        @pl.when(h < heads)
        def _():
            intra(h, Q, K, (0, V), (3, G))
            stage_totals(h)

        pl.when(h > 0)(lambda: stage_finish(h - 1))
        pl.when(h < heads)(lambda: intra(h, G, V, (1, K), (2, Q)))
        return carry

    lax.fori_loop(0, heads + 1, turn, 0)

    def drain(h, carry):
        for a in range(4):
            wait_bytes(buf.at[a, h, pl.ds(0, tok - part), :], a_send.at[a, h])
        wait_bytes(y_in.at[h, pl.ds(0, ny - 1)], y_send.at[h])
        wait_bytes(z_in.at[h, pl.ds(0, nz - 1)], z_send.at[h])
        wait_bytes(y_in.at[h, pl.ds(0, ny - 1)], p_send.at[h])
        return carry

    lax.fori_loop(0, heads, drain, 0)


def shards(nx, ny, nz, queries, keys, values, out_grad, doc_ids):
    part, width = queries.shape
    tok = part * nx
    heads = width // DH // nx
    rows = DH // ny
    docs = doc_ids.reshape(-1, 128)
    dma = pltpu.SemaphoreType.DMA
    return pl.pallas_call(
        functools.partial(kernel, nx, ny, nz, heads, tok),
        out_shape=[pltpu.VMEM((tok, heads * DH), BF16)] * 4,
        in_specs=[pl.BlockSpec(memory_space=pl.ANY)] * 5,
        out_specs=[pl.BlockSpec(memory_space=pltpu.VMEM)] * 4,
        scratch_shapes=[
            pltpu.VMEM((4, heads, tok, DH), BF16),
            pltpu.VMEM((4, heads, tok, DH), F32),
            pltpu.VMEM((tok, tok), BF16),
            pltpu.VMEM((tok, tok), BF16),
            pltpu.VMEM((4, tok, DH), BF16),
            pltpu.VMEM(docs.shape, jnp.int32),
            pltpu.SMEM(docs.shape, jnp.int32),
            pltpu.VMEM((heads, 2, DH, DH), BF16),
            pltpu.VMEM((heads, ny, 2, rows, DH), BF16),
            pltpu.VMEM((heads, 2, rows, DH), BF16),
            pltpu.VMEM((heads, nz, rows, DH), BF16),
            pltpu.VMEM((heads, ny, 2, rows, DH), BF16),
            pltpu.VMEM((heads, 2, DH, DH), BF16),
            dma((2,)),
            dma((4, heads)),
            dma((4, heads)),
            dma((4, heads)),
            dma((heads,)),
            dma((heads,)),
            dma((heads,)),
            dma((heads,)),
            dma((heads,)),
            dma((heads,)),
        ],
        compiler_params=pltpu.CompilerParams(
            collective_id=0, has_side_effects=True, vmem_limit_bytes=40 * 1024 * 1024
        ),
    )(queries, keys, values, out_grad, docs)


def solution(mesh):
    nx, blocks = mesh.shape["head"], mesh.shape["ctx"]
    ny = min(ROW, blocks)
    rows = P(("ctx", "head"), None)
    return jax.shard_map(
        functools.partial(shards, nx, ny, blocks // ny),
        mesh=mesh,
        in_specs=(rows, rows, rows, rows, P()),
        out_specs=(P("ctx", "head"),) * 4,
        check_vma=False,
    )
```

time: 568 us -> 72.4 us (0.13)
  the two profiles are of different devices: /device:TPU:2 before, /device:TPU:64 now
where the time goes in v1:
time: 72.4 us; the launch traced here: 72 us
  Pallas kernels  63.1 us (87%)
  local copies, waits for them, and re-layouts  8.24 us (11%)
    pallas_call x1, Pallas kernels, shards(): pl.pallas_call(functools.partial(kernel, nx, ny, nz, heads, tok), out_sha...  63.1 us
    unnamed x14, local copies, waits for them, and re-layouts  8.24 us

profile of v1, /device:TPU:64, one launch (start us, length us, event | category | flops | bytes accessed | tf_op | source)
XLA Modules:
  0.0 72.0 jit_solution(6916108673369017015)
XLA Ops:
  0.6 0.0 copy-start
  0.6 1.0 %copy-done = bf16[64,4096]{1,0:T(8,128)(2,1)S(1)} copy-done((bf16[64,4096]{1,0:T(8,128)(2,1)S(1)}, bf16[64,4096]{1,0:T(8,128)(2,1)}, u32[]{:S(2)}) %copy-start) | copy-done | bytes 524312
  1.7 0.0 copy-start.1
  1.7 1.0 %copy-done.1 = bf16[64,4096]{1,0:T(8,128)(2,1)S(1)} copy-done((bf16[64,4096]{1,0:T(8,128)(2,1)S(1)}, bf16[64,4096]{1,0:T(8,128)(2,1)}, u32[]{:S(2)}) %copy-start.1) | copy-done | bytes 524312
  2.7 0.0 copy-start.2
  2.7 1.0 %copy-done.2 = bf16[64,4096]{1,0:T(8,128)(2,1)S(1)} copy-done((bf16[64,4096]{1,0:T(8,128)(2,1)S(1)}, bf16[64,4096]{1,0:T(8,128)(2,1)}, u32[]{:S(2)}) %copy-start.2) | copy-done | bytes 524312
  3.8 0.0 copy-start.3
  3.8 1.0 %copy-done.3 = bf16[64,4096]{1,0:T(8,128)(2,1)S(1)} copy-done((bf16[64,4096]{1,0:T(8,128)(2,1)S(1)}, bf16[64,4096]{1,0:T(8,128)(2,1)}, u32[]{:S(2)}) %copy-start.3) | copy-done | bytes 524312
  4.8 0.0 copy-start.4
  4.8 0.9 %copy-done.4 = s32[32768]{0:T(1024)S(1)} copy-done((s32[32768]{0:T(1024)S(1)}, s32[32768]{0:T(1024)}, u32[]{:S(2)}) %copy-start.4) | copy-done | bytes 131096
  5.7 63.1 %shard_map.84 = (bf16[512,512]{1,0:T(8,128)(2,1)S(1)}, bf16[512,512]{1,0:T(8,128)(2,1)S(1)}, bf16[512,512]{1,0:T(8,128)(2,1)S(1)}, bf16[512,512]{1,0:T(8,128)(2,1)S(1)}) custom-call(bf16[64,4096]{1,0:T(8,128)(2,1)S(1)} %copy-done, bf16[64,4096]{1,0:T(8,128)(2,1)S(1)} %copy-done.1, bf16[64,4096]{1,0:T(8,128)(2,1)S(1)} %copy-done.2, ...), custom_call_target="tpu_custom_call" | custom-call | tf_op jit(solution)/shard_map/pallas_call | solution.py:262
  68.9 0.8 %copy.13 = bf16[512,512]{1,0:T(8,128)(2,1)} copy(bf16[512,512]{1,0:T(8,128)(2,1)S(1)} %get-tuple-element.4) | data formatting | bytes 1048576
  69.7 0.8 %copy.14 = bf16[512,512]{1,0:T(8,128)(2,1)} copy(bf16[512,512]{1,0:T(8,128)(2,1)S(1)} %get-tuple-element.5) | data formatting | bytes 1048576
  70.4 0.8 %copy.15 = bf16[512,512]{1,0:T(8,128)(2,1)} copy(bf16[512,512]{1,0:T(8,128)(2,1)S(1)} %get-tuple-element.6) | data formatting | bytes 1048576
  71.2 0.8 %copy.16 = bf16[512,512]{1,0:T(8,128)(2,1)} copy(bf16[512,512]{1,0:T(8,128)(2,1)S(1)} %get-tuple-element.7) | data formatting | bytes 1048576
Async XLA Ops:
  0.6 1.0 %copy-start = (bf16[64,4096]{1,0:T(8,128)(2,1)S(1)}, bf16[64,4096]{1,0:T(8,128)(2,1)}, u32[]{:S(2)}) copy-start(bf16[64,4096]{1,0:T(8,128)(2,1)} %q_ref.1) | copy-start | bytes 1572868
  1.7 1.0 %copy-start.1 = (bf16[64,4096]{1,0:T(8,128)(2,1)S(1)}, bf16[64,4096]{1,0:T(8,128)(2,1)}, u32[]{:S(2)}) copy-start(bf16[64,4096]{1,0:T(8,128)(2,1)} %k_ref.1) | copy-start | bytes 1572868
  2.7 1.0 %copy-start.2 = (bf16[64,4096]{1,0:T(8,128)(2,1)S(1)}, bf16[64,4096]{1,0:T(8,128)(2,1)}, u32[]{:S(2)}) copy-start(bf16[64,4096]{1,0:T(8,128)(2,1)} %v_ref.1) | copy-start | bytes 1572868
  3.8 1.0 %copy-start.3 = (bf16[64,4096]{1,0:T(8,128)(2,1)S(1)}, bf16[64,4096]{1,0:T(8,128)(2,1)}, u32[]{:S(2)}) copy-start(bf16[64,4096]{1,0:T(8,128)(2,1)} %g_ref.1) | copy-start | bytes 1572868
  4.8 0.9 %copy-start.4 = (s32[32768]{0:T(1024)S(1)}, s32[32768]{0:T(1024)}, u32[]{:S(2)}) copy-start(s32[32768]{0:T(1024)} %param.9) | copy-start | bytes 393220

commit v2 on v1

--- a/solution.py
+++ b/solution.py
@@ -33,7 +33,7 @@
 def kernel(
     nx, ny, nz, heads, tok,
     q_ref, k_ref, v_ref, g_ref, docs_ref,
-    att_ref, gq_ref, gk_ref, gv_ref,
+    out_ref,
     buf, acc, allow, allow_t, cols, docs_v, docs_s,
     st, y_in, z_out, z_in, p_out, held,
     docs_sem, own_sem, a_send, a_recv, y_send, y_recv, z_send, z_recv, p_send, p_recv,
@@ -221,25 +221,24 @@
         wait_bytes(y_in.at[h, pl.ds(0, ny - 1)], p_recv.at[h])
         to = pl.ds(pl.multiple_of(h * DH, DH), DH)
         state, gstate = held[h, 0], held[h, 1]
-        att_ref[:, to] = (acc[0, h] + nn(buf[Q, h] * cols[2], state)).astype(BF16)
-        gq_ref[:, to] = (acc[1, h] + nt(buf[G, h] * cols[2], state)).astype(BF16)
-        gk_ref[:, to] = (acc[2, h] + nt(buf[V, h] * cols[3], gstate)).astype(BF16)
-        gv_ref[:, to] = (acc[3, h] + nn(buf[K, h] * cols[3], gstate)).astype(BF16)
-
-    def turn(h, carry):
-        pl.when(h < heads)(lambda: stage_states(h))
-        pl.when(h > 0)(lambda: stage_prefix(h - 1))
-
-        @pl.when(h < heads)
+        out_ref[0, :, to] = (acc[0, h] + nn(buf[Q, h] * cols[2], state)).astype(BF16)
+        out_ref[1, :, to] = (acc[1, h] + nt(buf[G, h] * cols[2], state)).astype(BF16)
+        out_ref[2, :, to] = (acc[2, h] + nt(buf[V, h] * cols[3], gstate)).astype(BF16)
+        out_ref[3, :, to] = (acc[3, h] + nn(buf[K, h] * cols[3], gstate)).astype(BF16)
+
+    def turn(t, carry):
+        @pl.when(t < heads)
         def _():
-            intra(h, Q, K, (0, V), (3, G))
-            stage_totals(h)
-
-        pl.when(h > 0)(lambda: stage_finish(h - 1))
-        pl.when(h < heads)(lambda: intra(h, G, V, (1, K), (2, Q)))
+            stage_states(t)
+            intra(t, Q, K, (0, V), (3, G))
+            intra(t, G, V, (1, K), (2, Q))
+
+        pl.when(t > 1)(lambda: stage_finish(t - 2))
+        pl.when((t > 0) & (t <= heads))(lambda: stage_prefix(t - 1))
+        pl.when(t < heads)(lambda: stage_totals(t))
         return carry
 
-    lax.fori_loop(0, heads + 1, turn, 0)
+    lax.fori_loop(0, heads + 2, turn, 0)
 
     def drain(h, carry):
         for a in range(4):
@@ -252,18 +251,31 @@
     lax.fori_loop(0, heads, drain, 0)
 
 
+def write_out(*refs):
+    sems = refs[8]
+    copies = [pltpu.make_async_copy(refs[i], refs[i + 4], sems.at[i]) for i in range(4)]
+    for copy in copies:
+        copy.start()
+    for copy in copies:
+        copy.wait()
+
+
 def shards(nx, ny, nz, queries, keys, values, out_grad, doc_ids):
     part, width = queries.shape
     tok = part * nx
     heads = width // DH // nx
     rows = DH // ny
     docs = doc_ids.reshape(-1, 128)
+    queries, keys, values, out_grad, docs = (
+        pltpu.with_memory_space_constraint(x, pltpu.HBM)
+        for x in (queries, keys, values, out_grad, docs)
+    )
     dma = pltpu.SemaphoreType.DMA
-    return pl.pallas_call(
+    results = pl.pallas_call(
         functools.partial(kernel, nx, ny, nz, heads, tok),
-        out_shape=[pltpu.VMEM((tok, heads * DH), BF16)] * 4,
-        in_specs=[pl.BlockSpec(memory_space=pl.ANY)] * 5,
-        out_specs=[pl.BlockSpec(memory_space=pltpu.VMEM)] * 4,
+        out_shape=pltpu.VMEM((4, tok, heads * DH), BF16),
+        in_specs=[pl.BlockSpec(memory_space=pltpu.HBM)] * 5,
+        out_specs=pl.BlockSpec(memory_space=pltpu.VMEM),
         scratch_shapes=[
             pltpu.VMEM((4, heads, tok, DH), BF16),
             pltpu.VMEM((4, heads, tok, DH), F32),
@@ -293,6 +305,7 @@
             collective_id=0, has_side_effects=True, vmem_limit_bytes=40 * 1024 * 1024
         ),
     )(queries, keys, values, out_grad, docs)
+    return tuple(results[i] for i in range(4))
 
 
 def solution(mesh):

time: 72.4 us -> 58.6 us (0.81)
  the two profiles are of different devices: /device:TPU:64 before, /device:TPU:2 now
where the time goes in v2:
time: 58.6 us; the launch traced here: 58.5 us
  Pallas kernels  56.5 us (96%)
  local copies, waits for them, and re-layouts  1.35 us (2%)
  between operations  0.64 us (1%)
    pallas_call x1, Pallas kernels, shards(): pl.pallas_call(functools.partial(kernel, nx, ny, nz, heads, tok), out_sha...  56.5 us
    squeeze x1, local copies, waits for them, and re-layouts, shards(): return tuple((results[i] for i in range(4)))  1.35 us

profile of v2, /device:TPU:2, one launch (start us, length us, event | category | flops | bytes accessed | tf_op | source)
XLA Modules:
  0.0 58.5 jit_solution(1974564694548008492)
XLA Ops:
  0.6 56.5 %shard_map.84 = bf16[4,512,512]{2,1,0:T(8,128)(2,1)S(1)} custom-call(bf16[64,4096]{1,0:T(8,128)(2,1)} %q_ref.1, bf16[64,4096]{1,0:T(8,128)(2,1)} %k_ref.1, bf16[64,4096]{1,0:T(8,128)(2,1)} %v_ref.1, bf16[64,4096]{1,0:T(8,128)(2,1)} %g_ref.1, s32[256,128]{1,0:T(8,128)} %bitcast.9), custom_call_target="tpu_custom_call" | custom-call | tf_op jit(solution)/shard_map/pallas_call | solution.py:274
  57.1 1.3 %slice_bitcast_fusion = (bf16[512,512]{1,0:T(8,128)(2,1)}, bf16[512,512]{1,0:T(8,128)(2,1)}, bf16[512,512]{1,0:T(8,128)(2,1)}, bf16[512,512]{1,0:T(8,128)(2,1)}) fusion(bf16[4,512,512]{2,1,0:T(8,128)(2,1)S(1)} %shard_map.84), kind=kLoop, calls=%fused_computation | loop fusion | bytes 4194304 | tf_op jit(solution)/shard_map/squeeze | solution.py:308

commit v3 on v2

v3 whole, which is shorter than its diff:
```python
import functools

import jax
import jax.numpy as jnp
from jax import lax
from jax.experimental import pallas as pl
from jax.experimental.pallas import tpu as pltpu
from jax.sharding import PartitionSpec as P

DH = 128
ROW = 8
GROUP = 1
MESH = pl.DeviceIdType.MESH
F32, BF16 = jnp.float32, jnp.bfloat16
K, V, Q, G = range(4)


def nt(a, b):
    return lax.dot_general(a, b, (((1,), (1,)), ((), ())), preferred_element_type=F32)


def nn(a, b):
    return lax.dot_general(a, b, (((1,), (0,)), ((), ())), preferred_element_type=F32)


def tn(a, b):
    return lax.dot_general(a, b, (((0,), (0,)), ((), ())), preferred_element_type=F32)


def one_if(flag):
    return jnp.where(flag, F32(1.0), F32(0.0))


def wait_bytes(ref, sem):
    pltpu.make_async_copy(ref, ref, sem).wait()


def kernel(
    nx, ny, nz, heads, tok, group,
    q_ref, k_ref, v_ref, g_ref, docs_ref,
    out_ref,
    pair, buf, acc, allow, allow_t, cols, docs_v, docs_s, keeps,
    part_out, part_in, st, y_in, z_out, z_in, p_out, held,
    docs_sem, own_sem, pair_send, pair_recv, part_send, part_recv,
    mine_sem, tok_send, tok_recv, y_send, y_recv, z_send, z_recv, p_send, p_recv,
):
    ctx = lax.axis_index("ctx")
    me_x = lax.axis_index("head")
    me_z, me_y = ctx // ny, ctx % ny
    chip, core = me_x // 2, me_x % 2
    chips = nx // 2
    groups = heads // group
    part = tok // nx
    both = 2 * part
    rows = DH // ny
    per = tok // 128
    blocks = ny * nz
    wide = group * DH

    def at_chip(step):
        return {"head": lax.rem(chip + step, chips) * 2 + core}

    def y_peer(step):
        return lax.rem(me_y + step, ny)

    def at_y(step):
        return {"ctx": me_z * ny + y_peer(step)}

    def at_z(step):
        return {"ctx": lax.rem(me_z + step, nz) * ny + me_y}

    sibling = {"head": me_x + 1 - 2 * core}
    sources = (k_ref, v_ref, q_ref, g_ref)
    own_rows = pl.ds(pl.multiple_of(core * part, part), part)

    def columns(owner, first):
        return pl.ds(pl.multiple_of((owner * heads + first) * DH, DH), wide)

    docs_copies = [
        pltpu.make_async_copy(docs_ref, docs_s, docs_sem.at[0]),
        pltpu.make_async_copy(docs_ref, docs_v, docs_sem.at[1]),
    ]
    for copy in docs_copies:
        copy.start()
    for g in range(groups):
        for a in range(4):
            for c in range(chips):
                pltpu.make_async_copy(
                    sources[a].at[:, columns(c * 2 + core, g * group)],
                    pair.at[a, c, own_rows, pl.ds(g * wide, wide)],
                    own_sem.at[g],
                ).start()

    barrier = pltpu.get_barrier_semaphore()
    peers = [sibling]
    peers += [at_chip(step) for step in range(1, chips)]
    peers += [at_y(step) for step in range(1, ny)]
    peers += [at_z(step) for step in range(1, nz)]
    for peer in peers:
        pl.semaphore_signal(barrier, inc=1, device_id=peer, device_id_type=MESH)
    pl.semaphore_wait(barrier, len(peers))

    for g in range(groups):
        for a in range(4):
            for c in range(chips):
                pltpu.make_async_remote_copy(
                    src_ref=sources[a].at[:, columns(c * 2 + 1 - core, g * group)],
                    dst_ref=pair.at[a, c, own_rows, pl.ds(g * wide, wide)],
                    send_sem=pair_send.at[g],
                    recv_sem=pair_recv.at[g],
                    device_id=sibling,
                    device_id_type=MESH,
                ).start()

    for copy in docs_copies:
        copy.wait()

    def last(block):
        return docs_s[block * per + per - 1, 127]

    def first(block):
        return docs_s[block * per, 0]

    prior_doc = jnp.where(ctx == 0, -1, last(jnp.maximum(ctx - 1, 0)))
    next_doc = jnp.where(ctx == blocks - 1, -1, first(jnp.minimum(ctx + 1, blocks - 1)))
    last_doc, first_doc = last(ctx), first(ctx)

    local = docs_v[pl.ds(pl.multiple_of(ctx * per, per), per), :]
    row_of = [jnp.broadcast_to(local[i : i + 1, :], (128, 128)) for i in range(per)]
    col_of = [r.T for r in row_of]
    for i in range(per):
        at = slice(i * 128, (i + 1) * 128)
        for n, doc in enumerate((last_doc, first_doc, prior_doc, next_doc)):
            cols[n, at, :] = one_if(col_of[i] == doc).astype(BF16)

    chip_rows = pl.ds(pl.multiple_of(chip * both, both), both)

    def send_partials(g):
        half = pair.at[:, :, pl.ds(0, part), pl.ds(0, wide)]
        wait_bytes(half, own_sem.at[g])
        wait_bytes(half, pair_recv.at[g])
        tail, lead = cols[0, chip_rows, :], cols[1, chip_rows, :]
        for c in range(chips):
            for i in range(group):
                at = pl.ds((g * group + i) * DH, DH)
                part_out[g, c, i, 0] = tn(pair[K, c, :, at] * tail, pair[V, c, :, at]).astype(BF16)
                part_out[g, c, i, 1] = tn(pair[Q, c, :, at] * lead, pair[G, c, :, at]).astype(BF16)
        for step in range(1, chips):
            pltpu.make_async_remote_copy(
                src_ref=part_out.at[g, lax.rem(chip + step, chips)],
                dst_ref=part_in.at[g, chip],
                send_sem=part_send.at[g],
                recv_sem=part_recv.at[g],
                device_id=at_chip(step),
                device_id_type=MESH,
            ).start()
        part_in[g, chip] = part_out[g, chip]

    for g in range(groups):
        send_partials(g)

    def send_tokens(h, carry):
        at = pl.ds(pl.multiple_of(h * DH, DH), DH)
        for a in range(4):
            for step in range(1, chips):
                pltpu.make_async_remote_copy(
                    src_ref=pair.at[a, lax.rem(chip + step, chips), :, at],
                    dst_ref=buf.at[a, chip_rows, at],
                    send_sem=tok_send.at[h],
                    recv_sem=tok_recv.at[h],
                    device_id=at_chip(step),
                    device_id_type=MESH,
                ).start()
            pltpu.make_async_copy(
                pair.at[a, chip, :, at], buf.at[a, chip_rows, at], mine_sem.at[h]
            ).start()
        return carry

    lax.fori_loop(0, heads, send_tokens, 0)

    t_pos = lax.broadcasted_iota(jnp.int32, (128, 128), 0)
    s_pos = lax.broadcasted_iota(jnp.int32, (128, 128), 1)
    for i in range(per):
        at = slice(i * 128, (i + 1) * 128)
        for j in range(per):
            to = slice(j * 128, (j + 1) * 128)
            same = col_of[i] == row_of[j]
            allow[at, to] = one_if(same & (t_pos + i * 128 >= s_pos + j * 128)).astype(BF16)
            allow_t[at, to] = one_if(same & (t_pos + i * 128 <= s_pos + j * 128)).astype(BF16)

    base = me_z * ny
    before, after = last(jnp.maximum(base - 1, 0)), first(jnp.minimum(base + ny, blocks - 1))
    for y in range(ny):
        at = base + y
        keeps[0, y] = one_if(last(at) == last(jnp.maximum(at - 1, 0)))
        keeps[1, y] = one_if(first(at) == first(jnp.minimum(at + 1, blocks - 1)))
    for z in range(nz):
        keeps[2, z] = one_if((z < me_z) & (last(z * ny + ny - 1) == before))
        keeps[3, z] = one_if((z > me_z) & (first(z * ny) == after))

    def stage_states(g):
        wait_bytes(part_in.at[g, pl.ds(0, chips - 1)], part_recv.at[g])
        for i in range(group):
            for n in range(2):
                total = part_in[g, 0, i, n].astype(F32)
                for c in range(1, chips):
                    total = total + part_in[g, c, i, n].astype(F32)
                st[g, i, n] = total.astype(BF16)
        for step in range(1, ny):
            slot = pl.multiple_of(y_peer(step) * rows, rows)
            pltpu.make_async_remote_copy(
                src_ref=st.at[g, :, :, pl.ds(slot, rows), :],
                dst_ref=y_in.at[g, me_y],
                send_sem=y_send.at[g],
                recv_sem=y_recv.at[g],
                device_id=at_y(step),
                device_id_type=MESH,
            ).start()
        y_in[g, me_y] = st[g, :, :, pl.ds(pl.multiple_of(me_y * rows, rows), rows), :]

    def stage_totals(g):
        wait_bytes(y_in.at[g, pl.ds(0, ny - 1)], y_recv.at[g])
        total = y_in[g, 0, :, 0].astype(F32)
        for y in range(1, ny):
            total = y_in[g, y, :, 0].astype(F32) + keeps[0, y] * total
        z_out[g, 0] = total.astype(BF16)
        total = y_in[g, ny - 1, :, 1].astype(F32)
        for y in reversed(range(ny - 1)):
            total = y_in[g, y, :, 1].astype(F32) + keeps[1, y] * total
        z_out[g, 1] = total.astype(BF16)
        for step in range(1, nz):
            pltpu.make_async_remote_copy(
                src_ref=z_out.at[g, (me_z + step) // nz],
                dst_ref=z_in.at[g, me_z],
                send_sem=z_send.at[g],
                recv_sem=z_recv.at[g],
                device_id=at_z(step),
                device_id_type=MESH,
            ).start()
        z_in[g, me_z] = jnp.zeros((group, rows, DH), BF16)

    def stage_prefix(g):
        wait_bytes(z_in.at[g, pl.ds(0, nz - 1)], z_recv.at[g])
        state = jnp.zeros((group, rows, DH), F32)
        gstate = jnp.zeros((group, rows, DH), F32)
        for z in range(nz):
            term = z_in[g, z].astype(F32)
            state = state + keeps[2, z] * term
            gstate = gstate + keeps[3, z] * term
        for y in range(ny):
            p_out[g, y, :, 0] = state.astype(BF16)
            if y < ny - 1:
                state = y_in[g, y, :, 0].astype(F32) + keeps[0, y] * state
        for y in reversed(range(ny)):
            p_out[g, y, :, 1] = gstate.astype(BF16)
            if y > 0:
                gstate = y_in[g, y, :, 1].astype(F32) + keeps[1, y] * gstate
        here = pl.ds(pl.multiple_of(me_y * rows, rows), rows)
        for step in range(1, ny):
            pltpu.make_async_remote_copy(
                src_ref=p_out.at[g, y_peer(step)],
                dst_ref=held.at[g, :, :, here, :],
                send_sem=p_send.at[g],
                recv_sem=p_recv.at[g],
                device_id=at_y(step),
                device_id_type=MESH,
            ).start()
        held[g, :, :, here, :] = p_out[g, me_y]

    arrival, phase = 3.0 * group, 5.5
    stages = [(g * arrival + n * phase, n, g) for g in range(groups) for n in range(3)]
    for _, n, g in sorted(stages):
        (stage_states, stage_totals, stage_prefix)[n](g)

    tile = min(256, tok)

    def scores(h, left, right, by_row, by_col):
        here = pl.ds(pl.multiple_of(h * DH, DH), DH)
        for i in range(tok // tile):
            at, upto = slice(i * tile, (i + 1) * tile), slice(0, (i + 1) * tile)
            s = nt(buf[left, at, here], buf[right, upto, here]).astype(BF16) * allow[at, upto]
            acc[by_row[0], h, at, :] = nn(s, buf[by_row[1], upto, here])
            onward = slice(i * tile, tok)
            s = nt(buf[right, at, here], buf[left, onward, here]).astype(BF16) * allow_t[at, onward]
            acc[by_col[0], h, at, :] = nn(s, buf[by_col[1], onward, here])

    def intra(h, carry):
        wait_bytes(buf.at[:, pl.ds(0, both), pl.ds(0, DH)], mine_sem.at[h])
        wait_bytes(buf.at[:, pl.ds(0, tok - both), pl.ds(0, DH)], tok_recv.at[h])
        scores(h, Q, K, (0, V), (3, G))
        scores(h, G, V, (1, K), (2, Q))
        return carry

    def finish(h, carry):
        g, i = h // group, h % group
        here = pl.ds(pl.multiple_of(h * DH, DH), DH)
        state, gstate = held[g, i, 0], held[g, i, 1]
        match, back = cols[2], cols[3]
        out_ref[0, :, here] = (acc[0, h] + nn(buf[Q, :, here] * match, state)).astype(BF16)
        out_ref[1, :, here] = (acc[1, h] + nt(buf[G, :, here] * match, state)).astype(BF16)
        out_ref[2, :, here] = (acc[2, h] + nt(buf[V, :, here] * back, gstate)).astype(BF16)
        out_ref[3, :, here] = (acc[3, h] + nn(buf[K, :, here] * back, gstate)).astype(BF16)
        return carry

    ahead = heads - group
    lax.fori_loop(0, heads - 1, intra, 0)
    for g in range(groups - 1):
        wait_bytes(y_in.at[g, pl.ds(0, ny - 1)], p_recv.at[g])
    lax.fori_loop(0, ahead, finish, 0)
    lax.fori_loop(heads - 1, heads, intra, 0)
    wait_bytes(y_in.at[groups - 1, pl.ds(0, ny - 1)], p_recv.at[groups - 1])
    lax.fori_loop(ahead, heads, finish, 0)

    for g in range(groups):
        wait_bytes(pair.at[:, :, pl.ds(0, part), pl.ds(0, wide)], pair_send.at[g])
        wait_bytes(part_in.at[g, pl.ds(0, chips - 1)], part_send.at[g])
        wait_bytes(y_in.at[g, pl.ds(0, ny - 1)], y_send.at[g])
        wait_bytes(z_in.at[g, pl.ds(0, nz - 1)], z_send.at[g])
        wait_bytes(y_in.at[g, pl.ds(0, ny - 1)], p_send.at[g])
    for h in range(heads):
        wait_bytes(buf.at[:, pl.ds(0, tok - both), pl.ds(0, DH)], tok_send.at[h])


def shards(nx, ny, nz, queries, keys, values, out_grad, doc_ids):
    part, width = queries.shape
    tok = part * nx
    heads = width // DH // nx
    group = min(GROUP, heads)
    groups = heads // group
    chips = nx // 2
    rows = DH // ny
    docs = doc_ids.reshape(-1, 128)
    operands = [
        pltpu.with_memory_space_constraint(x, pltpu.HBM)
        for x in (queries, keys, values, out_grad, docs)
    ]
    dma = pltpu.SemaphoreType.DMA
    results = pl.pallas_call(
        functools.partial(kernel, nx, ny, nz, heads, tok, group),
        out_shape=pltpu.VMEM((4, tok, heads * DH), BF16),
        in_specs=[pl.BlockSpec(memory_space=pltpu.HBM)] * 5,
        out_specs=pl.BlockSpec(memory_space=pltpu.VMEM),
        scratch_shapes=[
            pltpu.VMEM((4, chips, 2 * part, heads * DH), BF16),
            pltpu.VMEM((4, tok, heads * DH), BF16),
            pltpu.VMEM((4, heads, tok, DH), F32),
            pltpu.VMEM((tok, tok), BF16),
            pltpu.VMEM((tok, tok), BF16),
            pltpu.VMEM((4, tok, DH), BF16),
            pltpu.VMEM(docs.shape, jnp.int32),
            pltpu.SMEM(docs.shape, jnp.int32),
            pltpu.SMEM((4, max(ny, nz)), F32),
            pltpu.VMEM((groups, chips, group, 2, DH, DH), BF16),
            pltpu.VMEM((groups, chips, group, 2, DH, DH), BF16),
            pltpu.VMEM((groups, group, 2, DH, DH), BF16),
            pltpu.VMEM((groups, ny, group, 2, rows, DH), BF16),
            pltpu.VMEM((groups, 2, group, rows, DH), BF16),
            pltpu.VMEM((groups, nz, group, rows, DH), BF16),
            pltpu.VMEM((groups, ny, group, 2, rows, DH), BF16),
            pltpu.VMEM((groups, group, 2, DH, DH), BF16),
            dma((2,)),
            dma((groups,)),
            dma((groups,)),
            dma((groups,)),
            dma((groups,)),
            dma((groups,)),
            dma((heads,)),
            dma((heads,)),
            dma((heads,)),
            dma((groups,)),
            dma((groups,)),
            dma((groups,)),
            dma((groups,)),
            dma((groups,)),
            dma((groups,)),
        ],
        compiler_params=pltpu.CompilerParams(
            collective_id=0, has_side_effects=True, vmem_limit_bytes=40 * 1024 * 1024
        ),
    )(*operands)
    return tuple(results[i] for i in range(4))


def solution(mesh):
    nx, blocks = mesh.shape["head"], mesh.shape["ctx"]
    ny = min(ROW, blocks)
    rows = P(("ctx", "head"), None)
    return jax.shard_map(
        functools.partial(shards, nx, ny, blocks // ny),
        mesh=mesh,
        in_specs=(rows, rows, rows, rows, P()),
        out_specs=(P("ctx", "head"),) * 4,
        check_vma=False,
    )
```

time: 58.6 us -> 54.6 us (0.932)
  the two profiles are of different devices: /device:TPU:2 before, /device:TPU:1 now
where the time goes in v3:
time: 54.6 us; the launch traced here: 54.4 us
  Pallas kernels  52.5 us (96%)
  local copies, waits for them, and re-layouts  1.35 us (2%)
  between operations  0.64 us (1%)
    pallas_call x1, Pallas kernels, shards(): pl.pallas_call(functools.partial(kernel, nx, ny, nz, heads, tok, group),...  52.5 us
    squeeze x1, local copies, waits for them, and re-layouts, shards(): return tuple((results[i] for i in range(4)))  1.35 us

profile of v3, /device:TPU:1, one launch (start us, length us, event | category | flops | bytes accessed | tf_op | source)
XLA Modules:
  0.0 54.4 jit_solution(3212402384604006891)
XLA Ops:
  0.6 52.5 %shard_map.84 = bf16[4,512,512]{2,1,0:T(8,128)(2,1)S(1)} custom-call(bf16[64,4096]{1,0:T(8,128)(2,1)} %q_ref.1, bf16[64,4096]{1,0:T(8,128)(2,1)} %k_ref.1, bf16[64,4096]{1,0:T(8,128)(2,1)} %v_ref.1, bf16[64,4096]{1,0:T(8,128)(2,1)} %g_ref.1, s32[256,128]{1,0:T(8,128)} %bitcast.9), custom_call_target="tpu_custom_call" | custom-call | tf_op jit(solution)/shard_map/pallas_call | solution.py:338
  53.1 1.3 %slice_bitcast_fusion = (bf16[512,512]{1,0:T(8,128)(2,1)}, bf16[512,512]{1,0:T(8,128)(2,1)}, bf16[512,512]{1,0:T(8,128)(2,1)}, bf16[512,512]{1,0:T(8,128)(2,1)}) fusion(bf16[4,512,512]{2,1,0:T(8,128)(2,1)S(1)} %shard_map.84), kind=kLoop, calls=%fused_computation | loop fusion | bytes 4194304 | tf_op jit(solution)/shard_map/squeeze | solution.py:381

commit v4 on v3

--- a/solution.py
+++ b/solution.py
@@ -13,6 +13,7 @@
 MESH = pl.DeviceIdType.MESH
 F32, BF16 = jnp.float32, jnp.bfloat16
 K, V, Q, G = range(4)
+EARLY = (K,)
 
 
 def nt(a, b):
@@ -42,7 +43,7 @@
     pair, buf, acc, allow, allow_t, cols, docs_v, docs_s, keeps,
     part_out, part_in, st, y_in, z_out, z_in, p_out, held,
     docs_sem, own_sem, pair_send, pair_recv, part_send, part_recv,
-    mine_sem, tok_send, tok_recv, y_send, y_recv, z_send, z_recv, p_send, p_recv,
+    line_in, cross_in, mine_sem, tok_send, tok_recv, y_send, y_recv, z_send, z_recv, p_send, p_recv,
 ):
     ctx = lax.axis_index("ctx")
     me_x = lax.axis_index("head")
@@ -92,13 +93,25 @@
                 ).start()
 
     barrier = pltpu.get_barrier_semaphore()
-    peers = [sibling]
-    peers += [at_chip(step) for step in range(1, chips)]
-    peers += [at_y(step) for step in range(1, ny)]
-    peers += [at_z(step) for step in range(1, nz)]
-    for peer in peers:
-        pl.semaphore_signal(barrier, inc=1, device_id=peer, device_id_type=MESH)
-    pl.semaphore_wait(barrier, len(peers))
+
+    def greet(sem, peer):
+        pl.semaphore_signal(sem, inc=1, device_id=peer, device_id_type=MESH)
+
+    for step in range(1, chips):
+        greet(barrier, {"head": lax.rem(chip + step, chips) * 2})
+    pl.when(core == 1)(lambda: greet(barrier, sibling))
+    across = [at_y(step) for step in range(1, ny)] + [at_z(step) for step in range(1, nz)]
+    for peer in across:
+        greet(barrier, {**peer, "head": chip * 2 + 1})
+
+    @pl.when(core == 0)
+    def _():
+        pl.semaphore_wait(barrier, nx - 1)
+        greet(line_in, sibling)
+
+    @pl.when(core == 1)
+    def _():
+        pl.semaphore_wait(line_in, 1)
 
     for g in range(groups):
         for a in range(4):
@@ -112,6 +125,21 @@
                     device_id_type=MESH,
                 ).start()
 
+    chip_rows = pl.ds(pl.multiple_of(chip * both, both), both)
+    mine = pl.ds(pl.multiple_of(me_x * part, part), part)
+    for a in EARLY:
+        for step in range(1, chips):
+            there = lax.rem(chip + step, chips) * 2
+            for c in range(2):
+                pltpu.make_async_remote_copy(
+                    src_ref=sources[a].at[:, pl.ds(pl.multiple_of((there + c) * heads * DH, DH), DH)],
+                    dst_ref=buf.at[a, mine, pl.ds(0, DH)],
+                    send_sem=tok_send.at[0],
+                    recv_sem=tok_recv.at[0],
+                    device_id={"head": there + c},
+                    device_id_type=MESH,
+                ).start()
+
     for copy in docs_copies:
         copy.wait()
 
@@ -133,7 +161,6 @@
         for n, doc in enumerate((last_doc, first_doc, prior_doc, next_doc)):
             cols[n, at, :] = one_if(col_of[i] == doc).astype(BF16)
 
-    chip_rows = pl.ds(pl.multiple_of(chip * both, both), both)
 
     def send_partials(g):
         half = pair.at[:, :, pl.ds(0, part), pl.ds(0, wide)]
@@ -159,10 +186,10 @@
     for g in range(groups):
         send_partials(g)
 
-    def send_tokens(h, carry):
-        at = pl.ds(pl.multiple_of(h * DH, DH), DH)
+    def send_tokens(h, done=()):
+        at = pl.ds(h * DH, DH)
         for a in range(4):
-            for step in range(1, chips):
+            for step in range(1, chips) if a not in done else ():
                 pltpu.make_async_remote_copy(
                     src_ref=pair.at[a, lax.rem(chip + step, chips), :, at],
                     dst_ref=buf.at[a, chip_rows, at],
@@ -174,9 +201,10 @@
             pltpu.make_async_copy(
                 pair.at[a, chip, :, at], buf.at[a, chip_rows, at], mine_sem.at[h]
             ).start()
-        return carry
-
-    lax.fori_loop(0, heads, send_tokens, 0)
+
+    send_tokens(0, EARLY)
+    for h in range(1, heads):
+        send_tokens(h)
 
     t_pos = lax.broadcasted_iota(jnp.int32, (128, 128), 0)
     s_pos = lax.broadcasted_iota(jnp.int32, (128, 128), 1)
@@ -269,6 +297,16 @@
 
     arrival, phase = 3.0 * group, 5.5
     stages = [(g * arrival + n * phase, n, g) for g in range(groups) for n in range(3)]
+
+    @pl.when(core == 1)
+    def _():
+        pl.semaphore_wait(barrier, 2 * len(across))
+        greet(cross_in, sibling)
+
+    @pl.when(core == 0)
+    def _():
+        pl.semaphore_wait(cross_in, 1)
+
     for _, n, g in sorted(stages):
         (stage_states, stage_totals, stage_prefix)[n](g)
 
@@ -364,6 +402,8 @@
             dma((groups,)),
             dma((groups,)),
             dma((groups,)),
+            pltpu.SemaphoreType.REGULAR,
+            pltpu.SemaphoreType.REGULAR,
             dma((heads,)),
             dma((heads,)),
             dma((heads,)),

time: 54.6 us -> 50.1 us (0.918)
  Pallas kernels: 52.5 us -> 48 us
    pallas_call x1, Pallas kernels: 52.5 us -> 48 us  [shards(): pl.pallas_call(functools.partial(kernel, nx, ny, nz, heads, tok, group),...]
where the time goes in v4:
time: 50.1 us; the launch traced here: 49.9 us
  Pallas kernels  48 us (96%)
  local copies, waits for them, and re-layouts  1.35 us (3%)
  between operations  0.64 us (1%)
    pallas_call x1, Pallas kernels, shards(): pl.pallas_call(functools.partial(kernel, nx, ny, nz, heads, tok, group),...  48 us
    squeeze x1, local copies, waits for them, and re-layouts, shards(): return tuple((results[i] for i in range(4)))  1.35 us

profile of v4, /device:TPU:1, one launch (start us, length us, event | category | flops | bytes accessed | tf_op | source)
XLA Modules:
  0.0 49.9 jit_solution(13004951279889356768)
XLA Ops:
  0.6 48.0 %shard_map.84 = bf16[4,512,512]{2,1,0:T(8,128)(2,1)S(1)} custom-call(bf16[64,4096]{1,0:T(8,128)(2,1)} %q_ref.1, bf16[64,4096]{1,0:T(8,128)(2,1)} %k_ref.1, bf16[64,4096]{1,0:T(8,128)(2,1)} %v_ref.1, bf16[64,4096]{1,0:T(8,128)(2,1)} %g_ref.1, s32[256,128]{1,0:T(8,128)} %bitcast.9), custom_call_target="tpu_custom_call" | custom-call | tf_op jit(solution)/shard_map/pallas_call | solution.py:376
  48.6 1.3 %slice_bitcast_fusion = (bf16[512,512]{1,0:T(8,128)(2,1)}, bf16[512,512]{1,0:T(8,128)(2,1)}, bf16[512,512]{1,0:T(8,128)(2,1)}, bf16[512,512]{1,0:T(8,128)(2,1)}) fusion(bf16[4,512,512]{2,1,0:T(8,128)(2,1)S(1)} %shard_map.84), kind=kLoop, calls=%fused_computation | loop fusion | bytes 4194304 | tf_op jit(solution)/shard_map/squeeze | solution.py:421

commit v5 on v4

--- a/solution.py
+++ b/solution.py
@@ -10,6 +10,7 @@
 DH = 128
 ROW = 8
 GROUP = 1
+FIRST = 0
 MESH = pl.DeviceIdType.MESH
 F32, BF16 = jnp.float32, jnp.bfloat16
 K, V, Q, G = range(4)
@@ -33,16 +34,17 @@
 
 
 def wait_bytes(ref, sem):
-    pltpu.make_async_copy(ref, ref, sem).wait()
+    if 0 not in ref.shape:
+        pltpu.make_async_copy(ref, ref, sem).wait()
 
 
 def kernel(
     nx, ny, nz, heads, tok, group,
     q_ref, k_ref, v_ref, g_ref, docs_ref,
     out_ref,
-    pair, buf, acc, allow, allow_t, cols, docs_v, docs_s, keeps,
-    part_out, part_in, st, y_in, z_out, z_in, p_out, held,
-    docs_sem, own_sem, pair_send, pair_recv, part_send, part_recv,
+    pair, buf, acc, allow, allow_t, cols, docs_v, near_s, docs_s, keeps,
+    part_out, part_in, relay_in, relay_out, st, y_in, z_out, z_in, p_out, held,
+    docs_sem, own_sem, pair_send, pair_recv, part_send, part_recv, relay_send, relay_recv,
     line_in, cross_in, mine_sem, tok_send, tok_recv, y_send, y_recv, z_send, z_recv, p_send, p_recv,
 ):
     ctx = lax.axis_index("ctx")
@@ -58,8 +60,11 @@
     blocks = ny * nz
     wide = group * DH
 
+    def chip_at(step):
+        return lax.rem(chip + step, chips)
+
     def at_chip(step):
-        return {"head": lax.rem(chip + step, chips) * 2 + core}
+        return {"head": chip_at(step) * 2 + core}
 
     def y_peer(step):
         return lax.rem(me_y + step, ny)
@@ -77,9 +82,11 @@
     def columns(owner, first):
         return pl.ds(pl.multiple_of((owner * heads + first) * DH, DH), wide)
 
+    row_docs = pl.ds(pl.multiple_of(me_z * ny * per, ny * per), ny * per)
     docs_copies = [
-        pltpu.make_async_copy(docs_ref, docs_s, docs_sem.at[0]),
-        pltpu.make_async_copy(docs_ref, docs_v, docs_sem.at[1]),
+        pltpu.make_async_copy(docs_ref.at[row_docs], near_s, docs_sem.at[0]),
+        pltpu.make_async_copy(docs_ref.at[row_docs], docs_v, docs_sem.at[1]),
+        pltpu.make_async_copy(docs_ref, docs_s, docs_sem.at[2]),
     ]
     for copy in docs_copies:
         copy.start()
@@ -98,18 +105,18 @@
         pl.semaphore_signal(sem, inc=1, device_id=peer, device_id_type=MESH)
 
     for step in range(1, chips):
-        greet(barrier, {"head": lax.rem(chip + step, chips) * 2})
-    pl.when(core == 1)(lambda: greet(barrier, sibling))
+        greet(barrier, {"head": lax.rem(chip + step, chips) * 2 + 1})
+    pl.when(core == 0)(lambda: greet(barrier, sibling))
     across = [at_y(step) for step in range(1, ny)] + [at_z(step) for step in range(1, nz)]
     for peer in across:
-        greet(barrier, {**peer, "head": chip * 2 + 1})
-
-    @pl.when(core == 0)
+        greet(barrier, {**peer, "head": chip * 2})
+
+    @pl.when(core == 1)
     def _():
         pl.semaphore_wait(barrier, nx - 1)
         greet(line_in, sibling)
 
-    @pl.when(core == 1)
+    @pl.when(core == 0)
     def _():
         pl.semaphore_wait(line_in, 1)
 
@@ -140,26 +147,18 @@
                     device_id_type=MESH,
                 ).start()
 
-    for copy in docs_copies:
+    for copy in docs_copies[:2]:
         copy.wait()
 
-    def last(block):
-        return docs_s[block * per + per - 1, 127]
-
-    def first(block):
-        return docs_s[block * per, 0]
-
-    prior_doc = jnp.where(ctx == 0, -1, last(jnp.maximum(ctx - 1, 0)))
-    next_doc = jnp.where(ctx == blocks - 1, -1, first(jnp.minimum(ctx + 1, blocks - 1)))
-    last_doc, first_doc = last(ctx), first(ctx)
-
-    local = docs_v[pl.ds(pl.multiple_of(ctx * per, per), per), :]
+    def mark(n, doc):
+        for i in range(per):
+            cols[n, i * 128 : (i + 1) * 128, :] = one_if(col_of[i] == doc).astype(BF16)
+
+    local = docs_v[pl.ds(pl.multiple_of(me_y * per, per), per), :]
     row_of = [jnp.broadcast_to(local[i : i + 1, :], (128, 128)) for i in range(per)]
     col_of = [r.T for r in row_of]
-    for i in range(per):
-        at = slice(i * 128, (i + 1) * 128)
-        for n, doc in enumerate((last_doc, first_doc, prior_doc, next_doc)):
-            cols[n, at, :] = one_if(col_of[i] == doc).astype(BF16)
+    mark(0, near_s[me_y * per + per - 1, 127])
+    mark(1, near_s[me_y * per, 0])
 
 
     def send_partials(g):
@@ -172,39 +171,69 @@
                 at = pl.ds((g * group + i) * DH, DH)
                 part_out[g, c, i, 0] = tn(pair[K, c, :, at] * tail, pair[V, c, :, at]).astype(BF16)
                 part_out[g, c, i, 1] = tn(pair[Q, c, :, at] * lead, pair[G, c, :, at]).astype(BF16)
-        for step in range(1, chips):
-            pltpu.make_async_remote_copy(
-                src_ref=part_out.at[g, lax.rem(chip + step, chips)],
-                dst_ref=part_in.at[g, chip],
+        for n in range(2):
+            near, far = (1, chips - 1) if n == 0 else (chips - 1, 1)
+            pltpu.make_async_remote_copy(
+                src_ref=part_out.at[g, chip_at(2), :, n],
+                dst_ref=relay_in.at[g, n],
+                send_sem=part_send.at[g],
+                recv_sem=relay_recv.at[g],
+                device_id=at_chip(near),
+                device_id_type=MESH,
+            ).start()
+            pltpu.make_async_remote_copy(
+                src_ref=part_out.at[g, chip_at(far), :, n],
+                dst_ref=part_in.at[g, 0, :, n],
                 send_sem=part_send.at[g],
                 recv_sem=part_recv.at[g],
-                device_id=at_chip(step),
-                device_id_type=MESH,
-            ).start()
-        part_in[g, chip] = part_out[g, chip]
-
-    for g in range(groups):
-        send_partials(g)
-
-    def send_tokens(h, done=()):
+                device_id=at_chip(far),
+                device_id_type=MESH,
+            ).start()
+
+    def relay_partials(g):
+        wait_bytes(relay_in.at[g], relay_recv.at[g])
+        for n in range(2):
+            near = 1 if n == 0 else chips - 1
+            relay_out[g, n] = (
+                part_out[g, chip_at(near), :, n].astype(F32) + relay_in[g, n].astype(F32)
+            ).astype(BF16)
+            pltpu.make_async_remote_copy(
+                src_ref=relay_out.at[g, n],
+                dst_ref=part_in.at[g, 1, :, n],
+                send_sem=relay_send.at[g],
+                recv_sem=part_recv.at[g],
+                device_id=at_chip(near),
+                device_id_type=MESH,
+            ).start()
+
+    def send_tokens(h, arrays=range(4)):
         at = pl.ds(h * DH, DH)
-        for a in range(4):
-            for step in range(1, chips) if a not in done else ():
+        for a in arrays:
+            for step in range(1, chips):
                 pltpu.make_async_remote_copy(
-                    src_ref=pair.at[a, lax.rem(chip + step, chips), :, at],
+                    src_ref=pair.at[a, chip_at(step), :, at],
                     dst_ref=buf.at[a, chip_rows, at],
                     send_sem=tok_send.at[h],
                     recv_sem=tok_recv.at[h],
                     device_id=at_chip(step),
                     device_id_type=MESH,
                 ).start()
+
+    for g in range(groups):
+        send_partials(g)
+    rest = [a for a in range(4) if a not in EARLY]
+    send_tokens(0, rest[:FIRST])
+    for g in range(groups):
+        relay_partials(g)
+    send_tokens(0, rest[FIRST:])
+    for h in range(1, heads):
+        send_tokens(h)
+    for h in range(heads):
+        at = pl.ds(h * DH, DH)
+        for a in range(4):
             pltpu.make_async_copy(
                 pair.at[a, chip, :, at], buf.at[a, chip_rows, at], mine_sem.at[h]
             ).start()
-
-    send_tokens(0, EARLY)
-    for h in range(1, heads):
-        send_tokens(h)
 
     t_pos = lax.broadcasted_iota(jnp.int32, (128, 128), 0)
     s_pos = lax.broadcasted_iota(jnp.int32, (128, 128), 1)
@@ -216,6 +245,17 @@
             allow[at, to] = one_if(same & (t_pos + i * 128 >= s_pos + j * 128)).astype(BF16)
             allow_t[at, to] = one_if(same & (t_pos + i * 128 <= s_pos + j * 128)).astype(BF16)
 
+    docs_copies[2].wait()
+
+    def last(block):
+        return docs_s[block * per + per - 1, 127]
+
+    def first(block):
+        return docs_s[block * per, 0]
+
+    mark(2, jnp.where(ctx == 0, -1, last(jnp.maximum(ctx - 1, 0))))
+    mark(3, jnp.where(ctx == blocks - 1, -1, first(jnp.minimum(ctx + 1, blocks - 1))))
+
     base = me_z * ny
     before, after = last(jnp.maximum(base - 1, 0)), first(jnp.minimum(base + ny, blocks - 1))
     for y in range(ny):
@@ -227,11 +267,11 @@
         keeps[3, z] = one_if((z > me_z) & (first(z * ny) == after))
 
     def stage_states(g):
-        wait_bytes(part_in.at[g, pl.ds(0, chips - 1)], part_recv.at[g])
+        wait_bytes(part_in.at[g], part_recv.at[g])
         for i in range(group):
             for n in range(2):
-                total = part_in[g, 0, i, n].astype(F32)
-                for c in range(1, chips):
+                total = part_out[g, chip, i, n].astype(F32)
+                for c in range(2):
                     total = total + part_in[g, c, i, n].astype(F32)
                 st[g, i, n] = total.astype(BF16)
         for step in range(1, ny):
@@ -295,15 +335,15 @@
             ).start()
         held[g, :, :, here, :] = p_out[g, me_y]
 
-    arrival, phase = 3.0 * group, 5.5
+    arrival, phase = 1.3 * group, 5.5
     stages = [(g * arrival + n * phase, n, g) for g in range(groups) for n in range(3)]
 
-    @pl.when(core == 1)
+    @pl.when(core == 0)
     def _():
         pl.semaphore_wait(barrier, 2 * len(across))
         greet(cross_in, sibling)
 
-    @pl.when(core == 0)
+    @pl.when(core == 1)
     def _():
         pl.semaphore_wait(cross_in, 1)
 
@@ -351,7 +391,8 @@
 
     for g in range(groups):
         wait_bytes(pair.at[:, :, pl.ds(0, part), pl.ds(0, wide)], pair_send.at[g])
-        wait_bytes(part_in.at[g, pl.ds(0, chips - 1)], part_send.at[g])
+        wait_bytes(part_in.at[g], part_send.at[g])
+        wait_bytes(relay_in.at[g], relay_send.at[g])
         wait_bytes(y_in.at[g, pl.ds(0, ny - 1)], y_send.at[g])
         wait_bytes(z_in.at[g, pl.ds(0, nz - 1)], z_send.at[g])
         wait_bytes(y_in.at[g, pl.ds(0, ny - 1)], p_send.at[g])
@@ -385,18 +426,23 @@
             pltpu.VMEM((tok, tok), BF16),
             pltpu.VMEM((tok, tok), BF16),
             pltpu.VMEM((4, tok, DH), BF16),
-            pltpu.VMEM(docs.shape, jnp.int32),
+            pltpu.VMEM((ny * tok // 128, 128), jnp.int32),
+            pltpu.SMEM((ny * tok // 128, 128), jnp.int32),
             pltpu.SMEM(docs.shape, jnp.int32),
             pltpu.SMEM((4, max(ny, nz)), F32),
             pltpu.VMEM((groups, chips, group, 2, DH, DH), BF16),
-            pltpu.VMEM((groups, chips, group, 2, DH, DH), BF16),
+            pltpu.VMEM((groups, 2, group, 2, DH, DH), BF16),
+            pltpu.VMEM((groups, 2, group, DH, DH), BF16),
+            pltpu.VMEM((groups, 2, group, DH, DH), BF16),
             pltpu.VMEM((groups, group, 2, DH, DH), BF16),
             pltpu.VMEM((groups, ny, group, 2, rows, DH), BF16),
             pltpu.VMEM((groups, 2, group, rows, DH), BF16),
             pltpu.VMEM((groups, nz, group, rows, DH), BF16),
             pltpu.VMEM((groups, ny, group, 2, rows, DH), BF16),
             pltpu.VMEM((groups, group, 2, DH, DH), BF16),
-            dma((2,)),
+            dma((3,)),
+            dma((groups,)),
+            dma((groups,)),
             dma((groups,)),
             dma((groups,)),
             dma((groups,)),

time: 50.1 us -> 47.2 us (0.942)
  Pallas kernels: 48 us -> 44.9 us
    pallas_call x1, Pallas kernels: 48 us -> 44.9 us  [shards(): pl.pallas_call(functools.partial(kernel, nx, ny, nz, heads, tok, group),...]
where the time goes in v5:
time: 47.2 us; the launch traced here: 46.9 us
  Pallas kernels  44.9 us (95%)
  local copies, waits for them, and re-layouts  1.35 us (3%)
  between operations  0.64 us (1%)
    pallas_call x1, Pallas kernels, shards(): pl.pallas_call(functools.partial(kernel, nx, ny, nz, heads, tok, group),...  44.9 us
    squeeze x1, local copies, waits for them, and re-layouts, shards(): return tuple((results[i] for i in range(4)))  1.35 us

profile of v5, /device:TPU:1, one launch (start us, length us, event | category | flops | bytes accessed | tf_op | source)
XLA Modules:
  0.0 46.9 jit_solution(12368282369672360143)
XLA Ops:
  0.6 44.9 %shard_map.84 = bf16[4,512,512]{2,1,0:T(8,128)(2,1)S(1)} custom-call(bf16[64,4096]{1,0:T(8,128)(2,1)} %q_ref.1, bf16[64,4096]{1,0:T(8,128)(2,1)} %k_ref.1, bf16[64,4096]{1,0:T(8,128)(2,1)} %v_ref.1, bf16[64,4096]{1,0:T(8,128)(2,1)} %g_ref.1, s32[256,128]{1,0:T(8,128)} %bitcast.9), custom_call_target="tpu_custom_call" | custom-call | tf_op jit(solution)/shard_map/pallas_call | solution.py:417
  45.6 1.3 %slice_bitcast_fusion = (bf16[512,512]{1,0:T(8,128)(2,1)}, bf16[512,512]{1,0:T(8,128)(2,1)}, bf16[512,512]{1,0:T(8,128)(2,1)}, bf16[512,512]{1,0:T(8,128)(2,1)}) fusion(bf16[4,512,512]{2,1,0:T(8,128)(2,1)S(1)} %shard_map.84), kind=kLoop, calls=%fused_computation | loop fusion | bytes 4194304 | tf_op jit(solution)/shard_map/squeeze | solution.py:467

commit v6 on v5

--- a/solution.py
+++ b/solution.py
@@ -31,6 +31,10 @@
 
 def one_if(flag):
     return jnp.where(flag, F32(1.0), F32(0.0))
+
+
+def far_first(count):
+    return sorted(range(1, count), key=lambda step: -min(step, count - step))
 
 
 def wait_bytes(ref, sem):
@@ -53,6 +57,8 @@
     chip, core = me_x // 2, me_x % 2
     chips = nx // 2
     groups = heads // group
+    early = list(range(1, groups))
+    turns = early + [0]
     part = tok // nx
     both = 2 * part
     rows = DH // ny
@@ -90,7 +96,7 @@
     ]
     for copy in docs_copies:
         copy.start()
-    for g in range(groups):
+    for g in turns:
         for a in range(4):
             for c in range(chips):
                 pltpu.make_async_copy(
@@ -120,7 +126,7 @@
     def _():
         pl.semaphore_wait(line_in, 1)
 
-    for g in range(groups):
+    for g in turns:
         for a in range(4):
             for c in range(chips):
                 pltpu.make_async_remote_copy(
@@ -142,7 +148,7 @@
                     src_ref=sources[a].at[:, pl.ds(pl.multiple_of((there + c) * heads * DH, DH), DH)],
                     dst_ref=buf.at[a, mine, pl.ds(0, DH)],
                     send_sem=tok_send.at[0],
-                    recv_sem=tok_recv.at[0],
+                    recv_sem=tok_recv.at[heads if a in (K, V) else 0],
                     device_id={"head": there + c},
                     device_id_type=MESH,
                 ).start()
@@ -161,10 +167,13 @@
     mark(1, near_s[me_y * per, 0])
 
 
-    def send_partials(g):
+    def wait_pair(g):
         half = pair.at[:, :, pl.ds(0, part), pl.ds(0, wide)]
         wait_bytes(half, own_sem.at[g])
         wait_bytes(half, pair_recv.at[g])
+
+    def send_partials(g):
+        wait_pair(g)
         tail, lead = cols[0, chip_rows, :], cols[1, chip_rows, :]
         for c in range(chips):
             for i in range(group):
@@ -214,16 +223,17 @@
                     src_ref=pair.at[a, chip_at(step), :, at],
                     dst_ref=buf.at[a, chip_rows, at],
                     send_sem=tok_send.at[h],
-                    recv_sem=tok_recv.at[h],
+                    recv_sem=tok_recv.at[heads if h == 0 and a in (K, V) else h],
                     device_id=at_chip(step),
                     device_id_type=MESH,
                 ).start()
 
-    for g in range(groups):
+    for g in early:
         send_partials(g)
+    wait_pair(0)
     rest = [a for a in range(4) if a not in EARLY]
     send_tokens(0, rest[:FIRST])
-    for g in range(groups):
+    for g in early:
         relay_partials(g)
     send_tokens(0, rest[FIRST:])
     for h in range(1, heads):
@@ -266,15 +276,28 @@
         keeps[2, z] = one_if((z < me_z) & (last(z * ny + ny - 1) == before))
         keeps[3, z] = one_if((z > me_z) & (first(z * ny) == after))
 
+    def wait_tokens(h):
+        wait_bytes(buf.at[:, pl.ds(0, both), pl.ds(0, DH)], mine_sem.at[h])
+        wait_bytes(buf.at[:, pl.ds(0, tok - both), pl.ds(0, DH)], tok_recv.at[h])
+
     def stage_states(g):
-        wait_bytes(part_in.at[g], part_recv.at[g])
-        for i in range(group):
-            for n in range(2):
-                total = part_out[g, chip, i, n].astype(F32)
-                for c in range(2):
-                    total = total + part_in[g, c, i, n].astype(F32)
-                st[g, i, n] = total.astype(BF16)
-        for step in range(1, ny):
+        if g in early:
+            wait_bytes(part_in.at[g], part_recv.at[g])
+            for i in range(group):
+                for n in range(2):
+                    total = part_out[g, chip, i, n].astype(F32)
+                    for c in range(2):
+                        total = total + part_in[g, c, i, n].astype(F32)
+                    st[g, i, n] = total.astype(BF16)
+        else:
+            for i in range(group):
+                at = pl.ds((g * group + i) * DH, DH)
+                wait_bytes(buf.at[:, pl.ds(0, both), pl.ds(0, DH)], mine_sem.at[0])
+                wait_bytes(buf.at[pl.ds(0, 2), pl.ds(0, tok - both), pl.ds(0, DH)], tok_recv.at[heads])
+                st[g, i, 0] = tn(buf[K, :, at] * cols[0], buf[V, :, at]).astype(BF16)
+                wait_bytes(buf.at[pl.ds(0, 2), pl.ds(0, tok - both), pl.ds(0, DH)], tok_recv.at[0])
+                st[g, i, 1] = tn(buf[Q, :, at] * cols[1], buf[G, :, at]).astype(BF16)
+        for step in far_first(ny):
             slot = pl.multiple_of(y_peer(step) * rows, rows)
             pltpu.make_async_remote_copy(
                 src_ref=st.at[g, :, :, pl.ds(slot, rows), :],
@@ -296,7 +319,7 @@
         for y in reversed(range(ny - 1)):
             total = y_in[g, y, :, 1].astype(F32) + keeps[1, y] * total
         z_out[g, 1] = total.astype(BF16)
-        for step in range(1, nz):
+        for step in far_first(nz):
             pltpu.make_async_remote_copy(
                 src_ref=z_out.at[g, (me_z + step) // nz],
                 dst_ref=z_in.at[g, me_z],
@@ -324,7 +347,7 @@
             if y > 0:
                 gstate = y_in[g, y, :, 1].astype(F32) + keeps[1, y] * gstate
         here = pl.ds(pl.multiple_of(me_y * rows, rows), rows)
-        for step in range(1, ny):
+        for step in far_first(ny):
             pltpu.make_async_remote_copy(
                 src_ref=p_out.at[g, y_peer(step)],
                 dst_ref=held.at[g, :, :, here, :],
@@ -334,21 +357,6 @@
                 device_id_type=MESH,
             ).start()
         held[g, :, :, here, :] = p_out[g, me_y]
-
-    arrival, phase = 1.3 * group, 5.5
-    stages = [(g * arrival + n * phase, n, g) for g in range(groups) for n in range(3)]
-
-    @pl.when(core == 0)
-    def _():
-        pl.semaphore_wait(barrier, 2 * len(across))
-        greet(cross_in, sibling)
-
-    @pl.when(core == 1)
-    def _():
-        pl.semaphore_wait(cross_in, 1)
-
-    for _, n, g in sorted(stages):
-        (stage_states, stage_totals, stage_prefix)[n](g)
 
     tile = min(256, tok)
 
@@ -363,41 +371,58 @@
             acc[by_col[0], h, at, :] = nn(s, buf[by_col[1], onward, here])
 
     def intra(h, carry):
-        wait_bytes(buf.at[:, pl.ds(0, both), pl.ds(0, DH)], mine_sem.at[h])
-        wait_bytes(buf.at[:, pl.ds(0, tok - both), pl.ds(0, DH)], tok_recv.at[h])
+        pl.when(h >= group)(lambda: wait_tokens(h))
         scores(h, Q, K, (0, V), (3, G))
         scores(h, G, V, (1, K), (2, Q))
         return carry
 
-    def finish(h, carry):
+    def finish(h):
         g, i = h // group, h % group
-        here = pl.ds(pl.multiple_of(h * DH, DH), DH)
+        if i == 0:
+            wait_bytes(y_in.at[g, pl.ds(0, ny - 1)], p_recv.at[g])
+        here = pl.ds(h * DH, DH)
         state, gstate = held[g, i, 0], held[g, i, 1]
         match, back = cols[2], cols[3]
         out_ref[0, :, here] = (acc[0, h] + nn(buf[Q, :, here] * match, state)).astype(BF16)
         out_ref[1, :, here] = (acc[1, h] + nt(buf[G, :, here] * match, state)).astype(BF16)
         out_ref[2, :, here] = (acc[2, h] + nt(buf[V, :, here] * back, gstate)).astype(BF16)
         out_ref[3, :, here] = (acc[3, h] + nn(buf[K, :, here] * back, gstate)).astype(BF16)
-        return carry
-
-    ahead = heads - group
-    lax.fori_loop(0, heads - 1, intra, 0)
-    for g in range(groups - 1):
-        wait_bytes(y_in.at[g, pl.ds(0, ny - 1)], p_recv.at[g])
-    lax.fori_loop(0, ahead, finish, 0)
-    lax.fori_loop(heads - 1, heads, intra, 0)
-    wait_bytes(y_in.at[groups - 1, pl.ds(0, ny - 1)], p_recv.at[groups - 1])
-    lax.fori_loop(ahead, heads, finish, 0)
-
+
+    @pl.when(core == 0)
+    def _():
+        pl.semaphore_wait(barrier, 2 * len(across))
+        greet(cross_in, sibling)
+
+    @pl.when(core == 1)
+    def _():
+        pl.semaphore_wait(cross_in, 1)
+
+    for g in early:
+        stage_states(g)
+    stage_totals(early[0])
+    stage_states(0)
+    for g in early[1:] + [0]:
+        stage_totals(g)
+    lax.fori_loop(0, 2, intra, 0)
+    for g in turns:
+        stage_prefix(g)
+    lax.fori_loop(2, 3, intra, 0)
+    for h in (1, 2):
+        finish(h)
+    lax.fori_loop(3, 4, intra, 0)
     for g in range(groups):
         wait_bytes(pair.at[:, :, pl.ds(0, part), pl.ds(0, wide)], pair_send.at[g])
-        wait_bytes(part_in.at[g], part_send.at[g])
-        wait_bytes(relay_in.at[g], relay_send.at[g])
+        if g in early:
+            wait_bytes(part_in.at[g], part_send.at[g])
+            wait_bytes(relay_in.at[g], relay_send.at[g])
         wait_bytes(y_in.at[g, pl.ds(0, ny - 1)], y_send.at[g])
         wait_bytes(z_in.at[g, pl.ds(0, nz - 1)], z_send.at[g])
-        wait_bytes(y_in.at[g, pl.ds(0, ny - 1)], p_send.at[g])
     for h in range(heads):
         wait_bytes(buf.at[:, pl.ds(0, tok - both), pl.ds(0, DH)], tok_send.at[h])
+    for h in (3, 0):
+        finish(h)
+    for g in range(groups):
+        wait_bytes(y_in.at[g, pl.ds(0, ny - 1)], p_send.at[g])
 
 
 def shards(nx, ny, nz, queries, keys, values, out_grad, doc_ids):
@@ -452,7 +477,7 @@
             pltpu.SemaphoreType.REGULAR,
             dma((heads,)),
             dma((heads,)),
-            dma((heads,)),
+            dma((heads + 1,)),
             dma((groups,)),
             dma((groups,)),
             dma((groups,)),

time: 47.2 us -> 46.2 us (0.979); the launches traced: 46.9 us -> 45.4 us
  Pallas kernels: 44.9 us -> 43.4 us
    pallas_call x1, Pallas kernels: 44.9 us -> 43.4 us  [shards(): pl.pallas_call(functools.partial(kernel, nx, ny, nz, heads, tok, group),...]
where the time goes in v6:
time: 46.2 us; the launch traced here: 45.4 us
  Pallas kernels  43.4 us (94%)
  local copies, waits for them, and re-layouts  1.35 us (3%)
  between operations  0.64 us (1%)
    pallas_call x1, Pallas kernels, shards(): pl.pallas_call(functools.partial(kernel, nx, ny, nz, heads, tok, group),...  43.4 us
    squeeze x1, local copies, waits for them, and re-layouts, shards(): return tuple((results[i] for i in range(4)))  1.35 us

profile of v6, /device:TPU:1, one launch (start us, length us, event | category | flops | bytes accessed | tf_op | source)
XLA Modules:
  0.0 45.4 jit_solution(21339555650533634)
XLA Ops:
  0.6 43.4 %shard_map.84 = bf16[4,512,512]{2,1,0:T(8,128)(2,1)S(1)} custom-call(bf16[64,4096]{1,0:T(8,128)(2,1)} %q_ref.1, bf16[64,4096]{1,0:T(8,128)(2,1)} %k_ref.1, bf16[64,4096]{1,0:T(8,128)(2,1)} %v_ref.1, bf16[64,4096]{1,0:T(8,128)(2,1)} %g_ref.1, s32[256,128]{1,0:T(8,128)} %bitcast.9), custom_call_target="tpu_custom_call" | custom-call | tf_op jit(solution)/shard_map/pallas_call | solution.py:442
  44.1 1.3 %slice_bitcast_fusion = (bf16[512,512]{1,0:T(8,128)(2,1)}, bf16[512,512]{1,0:T(8,128)(2,1)}, bf16[512,512]{1,0:T(8,128)(2,1)}, bf16[512,512]{1,0:T(8,128)(2,1)}) fusion(bf16[4,512,512]{2,1,0:T(8,128)(2,1)S(1)} %shard_map.84), kind=kLoop, calls=%fused_computation | loop fusion | bytes 4194304 | tf_op jit(solution)/shard_map/squeeze | solution.py:492

commit v7 on v6

--- a/solution.py
+++ b/solution.py
@@ -10,7 +10,7 @@
 DH = 128
 ROW = 8
 GROUP = 1
-FIRST = 0
+FIRST = 1
 MESH = pl.DeviceIdType.MESH
 F32, BF16 = jnp.float32, jnp.bfloat16
 K, V, Q, G = range(4)

time: 46.2 us -> 45.7 us (0.989); the launches traced: 45.4 us -> 45.6 us
  no operation moved by 1% of the time
where the time goes in v7:
time: 45.7 us; the launch traced here: 45.6 us
  Pallas kernels  43.6 us (95%)
  local copies, waits for them, and re-layouts  1.35 us (3%)
  between operations  0.64 us (1%)
    pallas_call x1, Pallas kernels, shards(): pl.pallas_call(functools.partial(kernel, nx, ny, nz, heads, tok, group),...  43.6 us
    squeeze x1, local copies, waits for them, and re-layouts, shards(): return tuple((results[i] for i in range(4)))  1.35 us

profile of v7, /device:TPU:1, one launch (start us, length us, event | category | flops | bytes accessed | tf_op | source)
XLA Modules:
  0.0 45.6 jit_solution(13159116981358469099)
XLA Ops:
  0.6 43.6 %shard_map.84 = bf16[4,512,512]{2,1,0:T(8,128)(2,1)S(1)} custom-call(bf16[64,4096]{1,0:T(8,128)(2,1)} %q_ref.1, bf16[64,4096]{1,0:T(8,128)(2,1)} %k_ref.1, bf16[64,4096]{1,0:T(8,128)(2,1)} %v_ref.1, bf16[64,4096]{1,0:T(8,128)(2,1)} %g_ref.1, s32[256,128]{1,0:T(8,128)} %bitcast.9), custom_call_target="tpu_custom_call" | custom-call | tf_op jit(solution)/shard_map/pallas_call | solution.py:442
  44.2 1.3 %slice_bitcast_fusion = (bf16[512,512]{1,0:T(8,128)(2,1)}, bf16[512,512]{1,0:T(8,128)(2,1)}, bf16[512,512]{1,0:T(8,128)(2,1)}, bf16[512,512]{1,0:T(8,128)(2,1)}) fusion(bf16[4,512,512]{2,1,0:T(8,128)(2,1)S(1)} %shard_map.84), kind=kLoop, calls=%fused_computation | loop fusion | bytes 4194304 | tf_op jit(solution)/shard_map/squeeze | solution.py:492

commit v8 on v7

--- a/solution.py
+++ b/solution.py
@@ -223,7 +223,7 @@
                     src_ref=pair.at[a, chip_at(step), :, at],
                     dst_ref=buf.at[a, chip_rows, at],
                     send_sem=tok_send.at[h],
-                    recv_sem=tok_recv.at[heads if h == 0 and a in (K, V) else h],
+                    recv_sem=tok_recv.at[heads + h if a in ((K, V) if h == 0 else (G,)) else h],
                     device_id=at_chip(step),
                     device_id_type=MESH,
                 ).start()
@@ -275,10 +275,6 @@
     for z in range(nz):
         keeps[2, z] = one_if((z < me_z) & (last(z * ny + ny - 1) == before))
         keeps[3, z] = one_if((z > me_z) & (first(z * ny) == after))
-
-    def wait_tokens(h):
-        wait_bytes(buf.at[:, pl.ds(0, both), pl.ds(0, DH)], mine_sem.at[h])
-        wait_bytes(buf.at[:, pl.ds(0, tok - both), pl.ds(0, DH)], tok_recv.at[h])
 
     def stage_states(g):
         if g in early:
@@ -360,20 +356,33 @@
 
     tile = min(256, tok)
 
-    def scores(h, left, right, by_row, by_col):
+    def by_rows(h, left, right, to, by):
         here = pl.ds(pl.multiple_of(h * DH, DH), DH)
         for i in range(tok // tile):
             at, upto = slice(i * tile, (i + 1) * tile), slice(0, (i + 1) * tile)
             s = nt(buf[left, at, here], buf[right, upto, here]).astype(BF16) * allow[at, upto]
-            acc[by_row[0], h, at, :] = nn(s, buf[by_row[1], upto, here])
-            onward = slice(i * tile, tok)
+            acc[to, h, at, :] = nn(s, buf[by, upto, here])
+
+    def by_columns(h, left, right, to, by):
+        here = pl.ds(pl.multiple_of(h * DH, DH), DH)
+        for i in range(tok // tile):
+            at, onward = slice(i * tile, (i + 1) * tile), slice(i * tile, tok)
             s = nt(buf[right, at, here], buf[left, onward, here]).astype(BF16) * allow_t[at, onward]
-            acc[by_col[0], h, at, :] = nn(s, buf[by_col[1], onward, here])
+            acc[to, h, at, :] = nn(s, buf[by, onward, here])
 
     def intra(h, carry):
-        pl.when(h >= group)(lambda: wait_tokens(h))
-        scores(h, Q, K, (0, V), (3, G))
-        scores(h, G, V, (1, K), (2, Q))
+        @pl.when(h >= group)
+        def _():
+            wait_bytes(buf.at[:, pl.ds(0, both), pl.ds(0, DH)], mine_sem.at[h])
+            wait_bytes(buf.at[pl.ds(0, 3), pl.ds(0, tok - both), pl.ds(0, DH)], tok_recv.at[h])
+
+        by_rows(h, Q, K, 0, V)
+        pl.when(h >= group)(
+            lambda: wait_bytes(buf.at[G, pl.ds(0, tok - both), pl.ds(0, DH)], tok_recv.at[heads + h])
+        )
+        by_columns(h, Q, K, 3, G)
+        by_rows(h, G, V, 1, K)
+        by_columns(h, G, V, 2, Q)
         return carry
 
     def finish(h):
@@ -477,7 +486,7 @@
             pltpu.SemaphoreType.REGULAR,
             dma((heads,)),
             dma((heads,)),
-            dma((heads + 1,)),
+            dma((2 * heads,)),
             dma((groups,)),
             dma((groups,)),
             dma((groups,)),

time: 45.7 us -> 46.1 us (level); the launches traced: 45.6 us -> 45.4 us
  no operation moved by 1% of the time
where the time goes in v8:
time: 46.1 us; the launch traced here: 45.4 us
  Pallas kernels  43.4 us (94%)
  local copies, waits for them, and re-layouts  1.35 us (3%)
  between operations  0.64 us (1%)
    pallas_call x1, Pallas kernels, shards(): pl.pallas_call(functools.partial(kernel, nx, ny, nz, heads, tok, group),...  43.4 us
    squeeze x1, local copies, waits for them, and re-layouts, shards(): return tuple((results[i] for i in range(4)))  1.35 us

profile of v8, /device:TPU:1, one launch (start us, length us, event | category | flops | bytes accessed | tf_op | source)
XLA Modules:
  0.0 45.4 jit_solution(3124935553426446327)
XLA Ops:
  0.6 43.4 %shard_map.84 = bf16[4,512,512]{2,1,0:T(8,128)(2,1)S(1)} custom-call(bf16[64,4096]{1,0:T(8,128)(2,1)} %q_ref.1, bf16[64,4096]{1,0:T(8,128)(2,1)} %k_ref.1, bf16[64,4096]{1,0:T(8,128)(2,1)} %v_ref.1, bf16[64,4096]{1,0:T(8,128)(2,1)} %g_ref.1, s32[256,128]{1,0:T(8,128)} %bitcast.9), custom_call_target="tpu_custom_call" | custom-call | tf_op jit(solution)/shard_map/pallas_call | solution.py:451
  44.0 1.3 %slice_bitcast_fusion = (bf16[512,512]{1,0:T(8,128)(2,1)}, bf16[512,512]{1,0:T(8,128)(2,1)}, bf16[512,512]{1,0:T(8,128)(2,1)}, bf16[512,512]{1,0:T(8,128)(2,1)}) fusion(bf16[4,512,512]{2,1,0:T(8,128)(2,1)S(1)} %shard_map.84), kind=kLoop, calls=%fused_computation | loop fusion | bytes 4194304 | tf_op jit(solution)/shard_map/squeeze | solution.py:501
